TPU v7x, 256 devices: a whole 4x4x8 slice. The times are simulated.
256 devices in a mesh: gx: 16 (over y, x), gy: 16 (over z, core).
Axes of the slice: x: 4, y: 4, z: 8, core: 2. Of those that a mesh axis runs over, the one named last changes fastest.
Arguments:
- rhs: float32 [3, 128, 128, 512], P(None, 'gx', 'gy'), may hold values from -6 to 6
- stiffness: float32 [3, 128, 128, 512], P(None, 'gx', 'gy'), may hold values from 1 to 4
- couplings: bfloat16 [7, 3, 3, 128, 128, 512], P(None, None, None, 'gx', 'gy'), may hold values from -0.59765625 to 0.59765625
- tentative: bfloat16 [3, 6, 128, 128, 512], P(None, None, 'gx', 'gy'), may hold values from -1.1953125 to 1.1953125
- members: int32 [128, 128, 512], P('gx', 'gy'), may hold values from 0 to 1023
- coarse_stiffness: float32 [6, 262144], P(None, ('gx', 'gy')), may hold values from 1 to 4
- coarse_couplings: float32 [27, 36, 262144], P(None, None, ('gx', 'gy')), may hold values from -0.6 to 0.6
- coarse_columns: int32 [27, 262144], P(None, ('gx', 'gy')), may hold values from 0 to 2047
- send_lists: int32 [4, 65536], P(None, ('gx', 'gy')), may hold values from 0 to 1023
- coarse_tentative: float32 [36, 262144], P(None, ('gx', 'gy')), may hold values from -0.3125 to 0.3125
- coarse_members: int32 [262144], P(('gx', 'gy')), may hold values from 0 to 1
- coarsest_inverse: float32 [3072, 3072], P('gy', 'gx'), may hold values from -0.21875 to 0.21875
Outputs:
- solution: float32 [3, 128, 128, 512], P(None, 'gx', 'gy')
- coarse_solution: float32 [6, 262144], P(None, ('gx', 'gy'))
All inputs are finite; a program needn't handle non-finite values.
Results may differ from a plain program's by a relative error of at most 0.0015.
Values may be sent and summed in bfloat16 or wider, within the bound.
A program may use at most 128 MiB of HBM per device.

v0:
```python
import jax
import jax.numpy as jnp
from jax import lax
from jax.sharding import PartitionSpec as P

A2 = 2


damping = 0.6
smoothing = 0.5


def with_halo(cells, sides, width):
    for axis, dim in sides:
        count = lax.axis_size(axis)
        ends = count - 1
        head = lax.slice_in_dim(cells, 0, width, axis=dim)
        tail = lax.slice_in_dim(cells, cells.shape[dim] - width, cells.shape[dim], axis=dim)
        cells = jnp.concatenate(
            [
                lax.ppermute(tail, axis, [(i, (i + 1) % count) for i in range(ends)]),
                cells,
                lax.ppermute(head, axis, [((i + 1) % count, i) for i in range(ends)]),
            ],
            axis=dim,
        )
    return cells


def from_behind(value, axis, steps):
    count = lax.axis_size(axis)
    first, last = (max(0, -steps), min(count, count - steps))
    return lax.ppermute(value, axis, [(source, source + steps) for source in range(first, last)])


def stencil(padded, stiffness, couplings):
    padded = jnp.pad(padded, ((0, 0), (0, 0), (0, 0), (1, 1)))
    views = (
        padded[:, 1:-1, 1:-1, 1:-1],
        padded[:, :-2, 1:-1, 1:-1],
        padded[:, 2:, 1:-1, 1:-1],
        padded[:, 1:-1, :-2, 1:-1],
        padded[:, 1:-1, 2:, 1:-1],
        padded[:, 1:-1, 1:-1, :-2],
        padded[:, 1:-1, 1:-1, 2:],
    )
    total = stiffness * views[0]
    for offset in range(7):
        total = total + jnp.sum(couplings[offset].astype(jnp.float32) * views[offset][None], axis=1)
    return total


def fine_apply(field, stiffness, couplings):
    padded = with_halo(field, (("gx", 1), ("gy", 2)), 1)
    return stencil(padded, stiffness, couplings)


def coarse_apply(values, coarse_stiffness, coarse_couplings, coarse_columns, send_lists):
    outgoing = jnp.take(values, send_lists, axis=1)
    pieces = [values]
    for step_by, direction in ((1, 0), (-1, 1)):
        pieces.append(from_behind(outgoing[:, direction], "gx", step_by))
    for step_by, direction in ((1, 2), (-1, 3)):
        pieces.append(from_behind(outgoing[:, direction], "gy", step_by))
    extended = jnp.concatenate(pieces, axis=1)
    picked = jnp.take(extended, coarse_columns, axis=1)
    picked = jnp.transpose(picked, (1, 0, 2))
    blocks = coarse_couplings.reshape(coarse_couplings.shape[0], 6, 6, -1)
    return coarse_stiffness * values + jnp.sum(blocks * picked[:, None], axis=(0, 2))


def body(
    rhs,
    stiffness,
    couplings,
    tentative,
    members,
    coarse_stiffness,
    coarse_couplings,
    coarse_columns,
    send_lists,
    coarse_tentative,
    coarse_members,
    coarsest_inverse,
):
    first_count = coarse_stiffness.shape[1]

    def apply_fine(field):
        return fine_apply(field, stiffness, couplings)

    def apply_coarse(values):
        return coarse_apply(values, coarse_stiffness, coarse_couplings, coarse_columns, send_lists)

    x1 = damping * rhs / stiffness
    x2 = x1 + damping * (rhs - apply_fine(x1)) / stiffness
    r2 = rhs - apply_fine(x2)
    filtered = r2 - smoothing * apply_fine(r2 / stiffness)
    contrib = jnp.sum(tentative.astype(jnp.float32) * filtered[:, None], axis=0)
    coarse_rhs = jax.ops.segment_sum(
        contrib.reshape(6, -1).T, members.reshape(-1), num_segments=first_count
    ).T
    y1 = damping * coarse_rhs / coarse_stiffness
    s1 = coarse_rhs - apply_coarse(y1)
    blocks = coarse_tentative.reshape(6, 6, first_count)
    contrib2 = jnp.sum(blocks * s1[:, None], axis=0)
    summed = jax.ops.segment_sum(contrib2.T, coarse_members, num_segments=A2)
    local_rhs = summed.T.reshape(-1)
    own_count = local_rhs.shape[0]
    partial_value = jnp.dot(
        coarsest_inverse,
        lax.all_gather(local_rhs, "gy", axis=0, tiled=True),
        precision=lax.Precision.HIGHEST,
    )
    row_block = lax.psum(partial_value, "gx")
    full = lax.all_gather(row_block, "gy", axis=0, tiled=True)
    device_number = lax.axis_index("gx") * lax.axis_size("gy") + lax.axis_index("gy")
    own = lax.dynamic_slice_in_dim(full, device_number * own_count, own_count, 0).reshape(6, A2)
    spread = jnp.take(own, coarse_members, axis=1)
    y2 = y1 + jnp.sum(blocks * spread[None], axis=1)
    coarse_solution = y2 + damping * (coarse_rhs - apply_coarse(y2)) / coarse_stiffness
    picked = jnp.take(coarse_solution, members, axis=1)
    lifted = jnp.sum(tentative.astype(jnp.float32) * picked[None], axis=1)
    x3 = x2 + lifted - smoothing * apply_fine(lifted) / stiffness
    x4 = x3 + damping * (rhs - apply_fine(x3)) / stiffness
    solution = x4 + damping * (rhs - apply_fine(x4)) / stiffness
    return (solution, coarse_solution)


def solution(mesh):
    placed = (
        P(None, "gx", "gy", None),
        P(None, "gx", "gy", None),
        P(None, None, None, "gx", "gy", None),
        P(None, None, "gx", "gy", None),
        P("gx", "gy", None),
        P(None, ("gx", "gy")),
        P(None, None, ("gx", "gy")),
        P(None, ("gx", "gy")),
        P(None, ("gx", "gy")),
        P(None, ("gx", "gy")),
        P(("gx", "gy")),
        P("gy", "gx"),
    )
    return jax.shard_map(
        body,
        mesh=mesh,
        in_specs=placed,
        out_specs=(P(None, "gx", "gy", None), P(None, ("gx", "gy"))),
        check_vma=False,
    )
```

profile of v0, /device:TPU:9, one launch (start us, length us, event | category | flops | bytes accessed | tf_op | source)
XLA Modules:
  0.0 839.6 jit_solution(13033350841804693660)
XLA Ops:
  5.1 4.3 collective-permute-start.1
  10.6 5.2 collective-permute-start.2
  25.1 6.1 collective-permute-start.5
  33.1 5.0 collective-permute-done.4
  40.1 3.6 collective-permute-start.6
  58.6 5.6 collective-permute-start.10
  69.1 8.8 %copy.122 = f32[6,8,8,512]{0,3,2,1:T(8,128)} copy(f32[6,8,8,512]{3,2,1,0:T(8,128)S(1)} %fusion.2) | data formatting | bytes 1572864 | tf_op jit(solution)/shard_map/reshape | solution.py:100
  77.9 174.4 %scatter_custom_fusion = f32[1024,6]{1,0:T(8,128)S(1)} fusion(s32[32768]{0:T(1024)S(1)} %bitcast.141, f32[32768,6]{1,0:T(8,128)} %bitcast.134, f32[]{:T(128)} %constant.37.clone.1), kind=kCustom, calls=%fused_computation.188 | custom fusion | flops 196608 | bytes 25088 | tf_op jit(solution)/shard_map/scatter-add | solution.py:99
  261.6 4.3 collective-permute-start.14
  265.9 5.8 collective-permute-start.13
  272.8 91.4 %gather_fusion.3 = f32[27648,6]{1,0:T(8,128)} fusion(f32[6,2048]{0,1:T(8,128)S(1)} %copy.107, s32[27648]{0:T(1024)S(1)} %broadcast_clamp_fusion.1), kind=kCustom, calls=%fused_computation.1.clone | custom fusion | bytes 1437696 | tf_op jit(solution)/shard_map/jit(_take)/gather | solution.py:66
  364.2 10.3 %select_bitcast_fusion.2 = f32[27,6,1024]{1,2,0:T(8,128)} fusion(f32[27,1024,6]{2,1,0:T(8,128)} %bitcast.136, pred[27,1024]{1,0:T(8,128)(4,1)S(1)} %compare_and_fusion), kind=kLoop, calls=%fused_computation.10 | loop fusion | flops 165888 | bytes 1354752 | tf_op jit(solution)/shard_map/transpose | solution.py:67
  374.5 9.5 %copy.108 = f32[27,6,1024]{2,0,1:T(8,128)S(1)} copy(f32[27,6,1024]{1,2,0:T(8,128)} %select_bitcast_fusion.2) | data formatting | bytes 1327104 | tf_op jit(solution)/shard_map/transpose | solution.py:67
  384.0 4.9 fusion.1
  389.3 6.2 scatter_custom_fusion.1
  395.9 26.5 %all-reduce.6 = f32[192]{0:T(256)S(1)} all-reduce(f32[192]{0:T(256)S(1)} %dynamic-update-slice), channel_id=1, replica_groups=mesh['gx'=16,'gy'=16] {'gy'}, use_global_device_ids=true, to_apply=%add.6 | all-reduce | flops 192 | bytes 1536
  422.6 27.8 %psum.7 = f32[192]{0:T(256)S(1)} all-reduce(f32[192]{0:T(256)S(1)} %bitcast.145), channel_id=1, replica_groups=mesh['gx'=16,'gy'=16] {'gx'}, use_global_device_ids=true, to_apply=%region_27.30 | all-reduce | flops 192 | bytes 1536 | tf_op jit(solution)/shard_map/psum | solution.py:114
  450.7 51.0 %all-reduce.7 = f32[3072]{0:T(1024)S(1)} all-reduce(f32[3072]{0:T(1024)S(1)} %dynamic-update-slice.1), channel_id=1, replica_groups=mesh['gx'=16,'gy'=16] {'gy'}, use_global_device_ids=true, to_apply=%add.7 | all-reduce | flops 3072 | bytes 24576
  510.5 5.1 collective-permute-start.19
  517.6 5.8 collective-permute-start.17
  524.5 91.4 %gather_fusion.5 = f32[27648,6]{1,0:T(8,128)} fusion(f32[6,2048]{0,1:T(8,128)S(1)} %copy.117, s32[27648]{0:T(1024)S(1)} %broadcast_clamp_fusion.1), kind=kCustom, calls=%fused_computation.3.clone | custom fusion | bytes 1437696 | tf_op jit(solution)/shard_map/jit(_take)/gather | solution.py:66
  615.9 10.3 %select_bitcast_fusion.1 = f32[27,6,1024]{1,2,0:T(8,128)} fusion(f32[27,1024,6]{2,1,0:T(8,128)} %bitcast.135, pred[27,1024]{1,0:T(8,128)(4,1)S(1)} %compare_and_fusion), kind=kLoop, calls=%fused_computation.9 | loop fusion | flops 165888 | bytes 1354752 | tf_op jit(solution)/shard_map/transpose | solution.py:67
  626.2 9.5 %copy.118 = f32[27,6,1024]{2,0,1:T(8,128)S(1)} copy(f32[27,6,1024]{1,2,0:T(8,128)} %select_bitcast_fusion.1) | data formatting | bytes 1327104 | tf_op jit(solution)/shard_map/transpose | solution.py:67
  635.8 4.9 fusion
  641.0 108.2 %gather_fusion.1 = f32[32768,6]{1,0:T(8,128)} fusion(f32[6,1024]{0,1:T(8,128)S(1)} %copy.120, s32[32768]{0:T(1024)S(1)} %broadcast_clamp_fusion), kind=kCustom, calls=%fused_computation.5 | custom fusion | bytes 1703936 | tf_op jit(solution)/shard_map/jit(_take)/gather | solution.py:121
  749.3 11.9 %select_bitcast_fusion = f32[6,8,8,512]{0,3,2,1:T(8,128)} fusion(f32[8,8,512,6]{3,2,1,0:T(8,128)} %bitcast.133, pred[8,8,512]{2,1,0:T(8,128)(4,1)S(1)} %compare_and_fusion.1), kind=kLoop, calls=%fused_computation.8 | loop fusion | flops 196608 | bytes 1605632 | tf_op jit(solution)/shard_map/jit(_take)/select_n | solution.py:121
  761.2 10.1 %copy.121 = f32[6,8,8,512]{3,2,1,0:T(8,128)S(1)} copy(f32[6,8,8,512]{0,3,2,1:T(8,128)} %select_bitcast_fusion) | data formatting | bytes 1572864 | tf_op jit(solution)/shard_map/jit(_take)/select_n | solution.py:121
  772.8 5.7 collective-permute-start.21
  780.5 5.0 collective-permute-done.20
  785.6 5.0 collective-permute-start.23
  809.6 4.8 collective-permute-start.26
  829.0 5.8 collective-permute-start.30
  (185 shorter events, 102.3 us)
Async XLA Ops:
  1.9 7.6 collective-permute-start
  5.1 5.4 collective-permute-start.1
  10.6 7.2 collective-permute-start.2
  15.8 5.5 collective-permute-start.3
  25.1 8.1 collective-permute-start.5
  31.2 6.9 collective-permute-start.4
  38.2 5.6 collective-permute-start.7
  40.1 4.9 collective-permute-start.6
  47.7 5.3 collective-permute-start.9
  49.7 6.9 collective-permute-start.8
  56.7 7.6 collective-permute-start.11
  58.6 6.7 collective-permute-start.10
  255.8 15.8 %collective-permute-start.12 = (f32[6,256]{1,0:T(8,128)S(1)}, f32[6,256]{1,0:T(8,128)S(1)}, u32[]{:S(2)}, u32[]{:S(2)}) collective-permute-start(f32[6,256]{1,0:T(8,128)S(1)} %get-tuple-element.127), channel_id=1, source_target_pairs={{0,16},{16,32},{32,48},{48,64},{64,80},{80,96},{96,112},{112,128},... | collective-permute-start | bytes 18440 | tf_op jit(solution)/shard_map/ppermute | solution.py:33
  259.7 12.7 %collective-permute-start.15 = (f32[6,256]{1,0:T(8,128)S(1)}, f32[6,256]{1,0:T(8,128)S(1)}, u32[]{:S(2)}, u32[]{:S(2)}) collective-permute-start(f32[6,256]{1,0:T(8,128)S(1)} %get-tuple-element.124), channel_id=1, source_target_pairs={{1,0},{2,1},{3,2},{4,3},{5,4},{6,5},{7,6},{8,7},{9,8},{10,9},{11,1... | collective-permute-start | bytes 18440 | tf_op jit(solution)/shard_map/ppermute | solution.py:33
  261.6 10.8 %collective-permute-start.14 = (f32[6,256]{1,0:T(8,128)S(1)}, f32[6,256]{1,0:T(8,128)S(1)}, u32[]{:S(2)}, u32[]{:S(2)}) collective-permute-start(f32[6,256]{1,0:T(8,128)S(1)} %get-tuple-element.125), channel_id=1, source_target_pairs={{0,1},{1,2},{2,3},{3,4},{4,5},{5,6},{6,7},{7,8},{8,9},{9,10},{10,1... | collective-permute-start | bytes 18440 | tf_op jit(solution)/shard_map/ppermute | solution.py:33
  265.9 6.5 collective-permute-start.13
  508.5 14.8 %collective-permute-start.16 = (f32[6,256]{1,0:T(8,128)S(1)}, f32[6,256]{1,0:T(8,128)S(1)}, u32[]{:S(2)}, u32[]{:S(2)}) collective-permute-start(f32[6,256]{1,0:T(8,128)S(1)} %get-tuple-element.123), channel_id=1, source_target_pairs={{0,16},{16,32},{32,48},{48,64},{64,80},{80,96},{96,112},{112,128},... | collective-permute-start | bytes 18440 | tf_op jit(solution)/shard_map/ppermute | solution.py:33
  510.5 13.6 %collective-permute-start.19 = (f32[6,256]{1,0:T(8,128)S(1)}, f32[6,256]{1,0:T(8,128)S(1)}, u32[]{:S(2)}, u32[]{:S(2)}) collective-permute-start(f32[6,256]{1,0:T(8,128)S(1)} %get-tuple-element.120), channel_id=1, source_target_pairs={{1,0},{2,1},{3,2},{4,3},{5,4},{6,5},{7,6},{8,7},{9,8},{10,9},{11,1... | collective-permute-start | bytes 18440 | tf_op jit(solution)/shard_map/ppermute | solution.py:33
  515.7 8.5 %collective-permute-start.18 = (f32[6,256]{1,0:T(8,128)S(1)}, f32[6,256]{1,0:T(8,128)S(1)}, u32[]{:S(2)}, u32[]{:S(2)}) collective-permute-start(f32[6,256]{1,0:T(8,128)S(1)} %get-tuple-element.121), channel_id=1, source_target_pairs={{0,1},{1,2},{2,3},{3,4},{4,5},{5,6},{6,7},{7,8},{8,9},{9,10},{10,1... | collective-permute-start | bytes 18440 | tf_op jit(solution)/shard_map/ppermute | solution.py:33
  517.6 6.5 collective-permute-start.17
  772.8 7.7 collective-permute-start.21
  778.6 6.9 collective-permute-start.20
  785.6 6.9 collective-permute-start.23
  790.6 3.2 collective-permute-start.22
  797.5 5.3 collective-permute-start.25
  799.4 7.0 collective-permute-start.24
  806.5 7.9 collective-permute-start.27
  809.6 5.8 collective-permute-start.26
  818.1 5.3 collective-permute-start.29
  820.0 6.9 collective-permute-start.28
  827.1 7.8 collective-permute-start.31
  829.0 7.1 collective-permute-start.30
  (15 other events, 777.8 us)
where the time goes:
time: 847 us; the launch traced here: 840 us
  local copies, waits for them, and re-layouts  345 us (41%)
  other arithmetic  243 us (29%)
  starting transfers between devices  110 us (13%)
  blocking collectives  105 us (12%)
  waiting for transfers between devices  32.5 us (4%)
    gather x2, local copies, waits for them, and re-layouts, coarse_apply(): picked = jnp.take(extended, coarse_columns, axis=1)  183 us
    scatter-add x1, other arithmetic, body(): jax.ops.segment_sum(contrib.reshape(6, -1).T, members.reshape(-1), num_se...  174 us
    gather x1, local copies, waits for them, and re-layouts, body(): picked = jnp.take(coarse_solution, members, axis=1)  108 us
    unnamed x2, blocking collectives  77.5 us
    ppermute x12, starting transfers between devices, with_halo(): lax.ppermute(tail, axis, [(i, (i + 1) % count) for i in range(ends)])  44.1 us
    ppermute x12, starting transfers between devices, with_halo(): lax.ppermute(head, axis, [((i + 1) % count, i) for i in range(ends)])  37.6 us
    ppermute x8, starting transfers between devices, from_behind(): lax.ppermute(value, axis, [(source, source + steps) for source in range(f...  28.6 us
    psum x1, blocking collectives, body(): row_block = lax.psum(partial_value, 'gx')  27.8 us
  transfers between devices with their start and end apart: 32, of which 14 were waited for; matrix products, arithmetic and copies ran while one was open for 0% of the time, Pallas kernels for 0%

commit v1 on v0

v1 whole, which is shorter than its diff:
```python
import functools

import jax
import jax.numpy as jnp
from jax import lax
from jax.experimental import pallas as pl
from jax.experimental.pallas import tpu as pltpu
from jax.sharding import PartitionSpec as P

MESH = pl.DeviceIdType.MESH
F32 = jnp.float32
BF16 = jnp.bfloat16

FX = 8
FY = 8
NZ = 512
K = 27
A1 = 1024
H = 256
LANES = 128
FIELDS = 6

damping = 0.6
smoothing = 0.5


def lane_gather(table, index):
    dims = lax.GatherDimensionNumbers(
        offset_dims=(),
        collapsed_slice_dims=(1,),
        start_index_map=(1,),
        operand_batching_dims=(0,),
        start_indices_batching_dims=(0,),
    )
    return lax.gather(
        table, index[..., None], dims, slice_sizes=(1, 1), mode=lax.GatherScatterMode.PROMISE_IN_BOUNDS
    )


def pick(tables, index):
    low = index & (LANES - 1)
    parts = [lane_gather(table, low) for table in tables]
    bit = LANES
    while len(parts) > 1:
        upper = (index & bit) != 0
        parts = [jnp.where(upper, parts[at + 1], parts[at]) for at in range(0, len(parts), 2)]
        bit *= 2
    return parts[0]


def rows_of(piece, rows):
    sub = lax.broadcasted_iota(jnp.int32, (rows, 1), 0)
    first, last = (8 * piece) // 6, min((8 * piece + 7) // 6, 5)
    i = jnp.where(sub < 6 * (first + 1) - 8 * piece, first, last)
    return i, 8 * piece + sub - 6 * i


def kernel(
    nx,
    ny,
    rhs_h,
    stf_h,
    cpl_h,
    ten_h,
    mem_h,
    cst_h,
    ccp_h,
    col_h,
    snd_h,
    ctn_h,
    cmb_h,
    inv_h,
    sol,
    csol,
    rhs,
    stf,
    cpl,
    ten,
    mem,
    cst,
    ccp,
    col,
    snd,
    ctn,
    cmb,
    inv,
    wgt,
    field,
    yout,
    yin,
    acc,
    resid,
    nodes,
    crhs,
    y2,
    ext,
    cout,
    cacc,
    own_row,
    rows,
    part_row,
    parts,
    load_sem,
    fsend,
    frecv,
    csend,
    crecv,
    gsend,
    grecv,
    psend,
    precv,
):
    gx, gy = lax.axis_index("gx"), lax.axis_index("gy")
    near = (
        (gx > 0, {"gx": jnp.maximum(gx - 1, 0), "gy": gy}),
        (gx < nx - 1, {"gx": jnp.minimum(gx + 1, nx - 1), "gy": gy}),
        (gy > 0, {"gx": gx, "gy": jnp.maximum(gy - 1, 0)}),
        (gy < ny - 1, {"gx": gx, "gy": jnp.minimum(gy + 1, ny - 1)}),
    )

    loads = {}
    pairs = [("rhs", rhs_h, rhs), ("stf", stf_h, stf)]
    for offset in (0, 5, 6, 1, 2, 3, 4):
        pairs.append(("cpl%d" % offset, cpl_h.at[pl.ds(9 * offset, 9)], cpl.at[pl.ds(9 * offset, 9)]))
    pairs += [
        ("ten", ten_h, ten),
        ("mem", mem_h, mem),
        ("cst", cst_h, cst),
        ("snd", snd_h, snd),
        ("col", col_h, col),
        ("ccp", ccp_h, ccp),
        ("ctn", ctn_h, ctn),
        ("cmb", cmb_h, cmb),
        ("inv", inv_h, inv),
    ]
    for number, (name, source, target) in enumerate(pairs):
        loads[name] = pltpu.make_async_copy(source, target, load_sem.at[number])
        loads[name].start()

    barrier = pltpu.get_barrier_semaphore()
    for there, device in near:

        @pl.when(there)
        def _():
            pl.semaphore_signal(barrier, inc=1, device_id=device, device_id_type=MESH)

    def greet(step, carry):
        other = lax.rem(gy + step, ny)
        pl.semaphore_signal(barrier, inc=1, device_id={"gx": gx, "gy": other}, device_id_type=MESH)
        return carry

    lax.fori_loop(1, ny, greet, 0)

    def greet_sender(step, carry):
        other = lax.rem(gx + step, nx)

        @pl.when(jnp.logical_not(jnp.logical_and(other == gx, gx == gy)))
        def _():
            pl.semaphore_signal(barrier, inc=1, device_id={"gx": other, "gy": gx}, device_id_type=MESH)

        return carry

    lax.fori_loop(0, nx, greet_sender, 0)

    blank = jnp.zeros((FIELDS, 3, FY, NZ), F32)
    for side, (there, _) in enumerate(near):

        @pl.when(jnp.logical_not(there))
        def _():
            for number in range(FIELDS):
                if side < 2:
                    field[number, :, 0 if side == 0 else FX + 1] = blank[0]
                else:
                    yin[number, side - 2] = blank[0]
            for number in range(2):
                ext[number, :, pl.ds(A1 + H * side, H)] = jnp.zeros((8, H), F32)

    cacc[pl.ds(32, 8), :] = jnp.zeros((8, A1), F32)
    own_row[...] = jnp.zeros_like(own_row)
    part_row[...] = jnp.zeros_like(part_row)

    def halo(number, side):
        if side == 0:
            source, target, at = field.at[number, :, 1], field.at[number, :, FX + 1], 1
        elif side == 1:
            source, target, at = field.at[number, :, FX], field.at[number, :, 0], 0
        elif side == 2:
            source, target, at = yout.at[number, 0], yin.at[number, 1], 3
        else:
            source, target, at = yout.at[number, 1], yin.at[number, 0], 2
        return pltpu.make_async_remote_copy(
            src_ref=source,
            dst_ref=target,
            send_sem=fsend.at[number, side],
            recv_sem=frecv.at[number, at],
            device_id=near[side][1],
            device_id_type=MESH,
        )

    def send_halo(number, side):
        @pl.when(near[side][0])
        def _():
            halo(number, side).start()

    def wait_halo(number):
        for side in range(4):

            @pl.when(near[side][0])
            def _():
                halo(number, side ^ 1).wait_recv()

    def put_field(number, x, values):
        for c in range(3):
            field[number, c, x + 1] = values[c]
            yout[number, 0, c, pl.ds(x, 1), :] = values[c][0:1, :]
            yout[number, 1, c, pl.ds(x, 1), :] = values[c][FY - 1 : FY, :]

    def slabs(number, slab):
        slab(0)
        if number is not None:
            send_halo(number, 0)
        slab(FX - 1)
        if number is not None:
            send_halo(number, 1)

        def inner(x, carry):
            slab(x)
            return carry

        lax.fori_loop(1, FX - 1, inner, 0)
        if number is not None:
            send_halo(number, 2)
            send_halo(number, 3)

    def add(total, offset, x, j, view):
        for i in range(3):
            total[i] = total[i] + cpl[9 * offset + 3 * i + j, x].astype(F32) * view

    def inside(number):
        lane = lax.broadcasted_iota(jnp.int32, (FY, NZ), 1)

        def slab(x):
            total = [stf[i, x] * field[number, i, x + 1] for i in range(3)]
            for j in range(3):
                view = field[number, j, x + 1]
                add(total, 0, x, j, view)
                add(total, 5, x, j, jnp.where(lane == 0, 0.0, pltpu.roll(view, 1, axis=1)))
                add(total, 6, x, j, jnp.where(lane == NZ - 1, 0.0, pltpu.roll(view, NZ - 1, axis=1)))
                if not (isinstance(x, int) and x == 0):
                    add(total, 1, x, j, field[number, j, x])
                if not (isinstance(x, int) and x == FX - 1):
                    add(total, 2, x, j, field[number, j, x + 2])
            for i in range(3):
                acc[i, x] = total[i]

        slabs(None, slab)

    def outside(number, x):
        row = lax.broadcasted_iota(jnp.int32, (FY, NZ), 0)
        total = [acc[i, x] for i in range(3)]
        for j in range(3):
            view = field[number, j, x + 1]
            below = yin[number, 0, j, pl.ds(x, 1), :]
            above = yin[number, 1, j, pl.ds(x, 1), :]
            add(total, 3, x, j, jnp.where(row == 0, below, pltpu.roll(view, 1, axis=0)))
            add(total, 4, x, j, jnp.where(row == FY - 1, above, pltpu.roll(view, FY - 1, axis=0)))
            if isinstance(x, int) and x == 0:
                add(total, 1, x, j, field[number, j, 0])
            if isinstance(x, int) and x == FX - 1:
                add(total, 2, x, j, field[number, j, FX + 1])
        return total

    loads["rhs"].wait()
    loads["stf"].wait()

    def first(x):
        values = []
        for c in range(3):
            weight = 1.0 / stf[c, x]
            wgt[c, x] = weight
            values.append(damping * rhs[c, x] * weight)
        put_field(0, x, values)

    def first_slab(x, carry):
        first(x)
        return carry

    lax.fori_loop(0, FX, first_slab, 0)

    others = (
        sum(there.astype(jnp.int32) for there, _ in near) + (ny - 1) + nx - (gx == gy).astype(jnp.int32)
    )
    pl.semaphore_wait(barrier, others)
    for side in range(4):
        send_halo(0, side)

    for offset in (0, 5, 6, 1, 2, 3, 4):
        loads["cpl%d" % offset].wait()

    def smoothed(number, x):
        total = outside(number, x)
        return [
            field[number, c, x + 1] + damping * (rhs[c, x] - total[c]) * wgt[c, x] for c in range(3)
        ]

    inside(0)
    wait_halo(0)
    slabs(1, lambda x: put_field(1, x, smoothed(0, x)))

    def residual(x):
        total = outside(1, x)
        values = []
        for c in range(3):
            left = rhs[c, x] - total[c]
            resid[c, x] = left
            values.append(left * wgt[c, x])
        put_field(2, x, values)

    inside(1)
    wait_halo(1)
    slabs(2, residual)

    loads["ten"].wait()

    def restrict(x):
        total = outside(2, x)
        filtered = [resid[i, x] - smoothing * total[i] for i in range(3)]
        for c in range(6):
            value = ten[c, x].astype(F32) * filtered[0]
            for i in range(1, 3):
                value = value + ten[6 * i + c, x].astype(F32) * filtered[i]
            for t in range(NZ // LANES):
                part = value[:, LANES * t : LANES * (t + 1)]
                nodes[x, t, pl.ds(8 * c, 8), :] = part
                if c < 2:
                    nodes[x, t, pl.ds(8 * (c + 6), 8), :] = part

    inside(2)
    wait_halo(2)
    slabs(None, restrict)

    loads["mem"].wait()
    count = lax.broadcasted_iota(jnp.int32, (16, NZ), 0).astype(F32).astype(BF16)

    def sums(x, total):
        for y in range(FY):
            value = jnp.concatenate(
                [nodes[x, t, pl.ds(y, 8, stride=8), :] for t in range(NZ // LANES)], axis=1
            )
            rounded = value.astype(BF16).astype(F32)
            both = jnp.concatenate([rounded, value - rounded], axis=0).astype(BF16)
            index = jnp.broadcast_to(mem[x, pl.ds(y, 1), :], (16, NZ))
            low = (index & (LANES - 1)).astype(F32).astype(BF16)
            high = lax.shift_right_logical(index, 7).astype(F32).astype(BF16)
            zero = jnp.zeros((16, NZ), BF16)
            one = jnp.ones((16, NZ), BF16)
            left = jnp.concatenate([jnp.where(high == float(h), both, zero) for h in range(8)], axis=0)
            right = jnp.concatenate(
                [jnp.where(low == count + float(16 * k), one, zero) for k in range(8)], axis=0
            )
            total = total + lax.dot_general(
                left, right, (((1,), (1,)), ((), ())), preferred_element_type=F32
            )
        return total

    gathered = lax.fori_loop(0, FX, sums, jnp.zeros((LANES, LANES), F32))

    loads["cst"].wait()
    loads["snd"].wait()
    for h in range(8):
        span = pl.ds(LANES * h, LANES)
        crhs[:, span] = gathered[16 * h : 16 * h + 8] + gathered[16 * h + 8 : 16 * h + 16]
    cst8 = jnp.concatenate([cst[...], cst[0:2, :]], axis=0)
    ext[0, :, pl.ds(0, A1)] = damping * crhs[...] / cst8

    def coarse_halo(number, side):
        return pltpu.make_async_remote_copy(
            src_ref=cout.at[number, side],
            dst_ref=ext.at[number, :, pl.ds(A1 + H * side, H)],
            send_sem=csend.at[number, side],
            recv_sem=crecv.at[number, side],
            device_id=near[side ^ 1][1],
            device_id_type=MESH,
        )

    def send_coarse(number):
        tables = [ext[number, :, pl.ds(LANES * h, LANES)] for h in range(A1 // LANES)]
        for side in range(4):
            for t in range(H // LANES):
                index = jnp.broadcast_to(snd[side : side + 1, pl.ds(LANES * t, LANES)], (8, LANES))
                cout[number, side, :, pl.ds(LANES * t, LANES)] = pick(tables, index)

            @pl.when(near[side ^ 1][0])
            def _():
                coarse_halo(number, side).start()

    sub = lax.broadcasted_iota(jnp.int32, (8, LANES), 0)

    def coarse_apply(number):
        for side in range(4):

            @pl.when(near[side][0])
            def _():
                coarse_halo(number, side).wait_recv()

        def group(t, carry):
            span = pl.ds(pl.multiple_of(LANES * t, LANES), LANES)
            tables = [ext[number, :, pl.ds(LANES * h, LANES)] for h in range((A1 + 4 * H) // LANES)]
            total = [jnp.zeros((8 if piece < 4 else 4, LANES), F32) for piece in range(5)]
            columns = col[:, span]
            for k in range(K):
                base = pick(tables, jnp.broadcast_to(columns[k : k + 1], (8, LANES)))
                up2, by4, down2 = (pltpu.roll(base, by, axis=0) for by in (6, 4, 2))
                turned = (base, jnp.where(sub < 6, up2, by4), jnp.where(sub < 2, by4, down2))
                for piece in range(5):
                    size = 8 if piece < 4 else 4
                    block = ccp[k, pl.ds(8 * piece, size), span]
                    total[piece] = total[piece] + block * turned[piece % 3][:size]
            for piece in range(5):
                cacc[pl.ds(8 * piece, 8 if piece < 4 else 4), span] = total[piece]
            return carry

        lax.fori_loop(0, A1 // LANES, group, 0)

    fold_row = lax.broadcasted_iota(jnp.int32, (8, 40), 0)
    fold_col = lax.broadcasted_iota(jnp.int32, (8, 40), 1)
    fold_row = jnp.where(fold_row < 6, fold_row, fold_row - 6)
    fold = jnp.logical_and(fold_col >= 6 * fold_row, fold_col < 6 * fold_row + 6).astype(F32)

    def folded():
        return jnp.dot(fold, cacc[...], precision=lax.Precision.HIGHEST, preferred_element_type=F32)

    send_coarse(0)
    loads["col"].wait()
    loads["ccp"].wait()
    coarse_apply(0)
    s1 = crhs[...] - (cst8 * ext[0, :, pl.ds(0, A1)] + folded())

    loads["ctn"].wait()
    loads["cmb"].wait()
    loads["inv"].wait()
    lane = lax.broadcasted_iota(jnp.int32, (1, 2 * LANES), 1)
    upper = cmb[...] != 0
    row = jnp.zeros((1, 2 * LANES), F32)
    for piece in range(5):
        size = 8 if piece < 4 else 4
        i, c = rows_of(piece, size)
        first_i, last_i = (8 * piece) // 6, min((8 * piece + 7) // 6, 5)
        matching = jnp.where(i == first_i, s1[first_i : first_i + 1], s1[last_i : last_i + 1])
        product = ctn[pl.ds(8 * piece, size), :] * matching
        for a in range(2):
            kept = jnp.where(upper, product, 0.0) if a else jnp.where(upper, 0.0, product)
            total = jnp.sum(kept, axis=1, keepdims=True)
            place = 12 * gy + 2 * c + a
            row = row + jnp.sum(jnp.where(lane == place, total, 0.0), axis=0, keepdims=True)
    own_row[...] = row

    def to_row(step):
        other = lax.rem(gy + step, ny)
        return pltpu.make_async_remote_copy(
            src_ref=own_row,
            dst_ref=rows.at[gy],
            send_sem=gsend.at[other],
            recv_sem=grecv.at[gy],
            device_id={"gx": gx, "gy": other},
            device_id_type=MESH,
        )

    def from_row(other):
        return pltpu.make_async_remote_copy(
            src_ref=own_row,
            dst_ref=rows.at[other],
            send_sem=gsend.at[other],
            recv_sem=grecv.at[other],
            device_id={"gx": gx, "gy": other},
            device_id_type=MESH,
        )

    def send_row(step, carry):
        to_row(step).start()
        return carry

    lax.fori_loop(1, ny, send_row, 0)

    def take_row(step, carry):
        from_row(lax.rem(gy + step, ny)).wait_recv()
        return carry

    lax.fori_loop(1, ny, take_row, 0)
    rows[gy] = row
    entries = jnp.sum(rows[...], axis=0)
    block = inv.shape[1]
    values = jnp.broadcast_to(entries[:, :block], (8, block))
    product = lax.dot_general(
        values, inv[...], (((1,), (1,)), ((), ())), precision=lax.Precision.HIGHEST, preferred_element_type=F32
    )
    part_row[:, pl.ds(0, block)] = product[0:1]

    def to_part(other):
        return pltpu.make_async_remote_copy(
            src_ref=part_row,
            dst_ref=parts.at[gx],
            send_sem=psend.at[other],
            recv_sem=precv.at[gx],
            device_id={"gx": gy, "gy": other},
            device_id_type=MESH,
        )

    def from_part(other):
        return pltpu.make_async_remote_copy(
            src_ref=part_row,
            dst_ref=parts.at[other],
            send_sem=psend.at[other],
            recv_sem=precv.at[other],
            device_id={"gx": other, "gy": gx},
            device_id_type=MESH,
        )

    def other_part(other):
        return jnp.logical_not(jnp.logical_and(other == gy, gx == gy))

    def send_part(step, carry):
        other = lax.rem(gy + step, ny)

        @pl.when(other_part(other))
        def _():
            to_part(other).start()

        return carry

    lax.fori_loop(0, ny, send_part, 0)

    def take_part(step, carry):
        other = lax.rem(gx + step, nx)

        @pl.when(jnp.logical_not(jnp.logical_and(other == gx, gx == gy)))
        def _():
            from_part(other).wait_recv()

        return carry

    lax.fori_loop(0, nx, take_part, 0)

    @pl.when(gx == gy)
    def _():
        parts[gx] = part_row[...]

    coarsest = jnp.sum(parts[...], axis=0)

    for piece in range(5):
        size = 8 if piece < 4 else 4
        at = pl.ds(8 * piece, size)
        _, c = rows_of(piece, size)
        spread = [
            jnp.sum(jnp.where(lane == 12 * gy + 2 * c + a, coarsest, 0.0), axis=1, keepdims=True)
            for a in range(2)
        ]
        cacc[at, :] = ctn[at, :] * jnp.where(upper, spread[1], spread[0])
    ext[1, :, pl.ds(0, A1)] = ext[0, :, pl.ds(0, A1)] + folded()
    send_coarse(1)
    coarse_apply(1)
    solved = ext[1, :, pl.ds(0, A1)]
    solved = solved + damping * (crhs[...] - (cst8 * solved + folded())) / cst8
    y2[...] = solved
    csol[...] = solved[0:6]

    def lift(x):
        tables = [y2[:, pl.ds(LANES * h, LANES)] for h in range(A1 // LANES)]
        for y in range(FY):
            for t in range(NZ // LANES):
                span = pl.ds(LANES * t, LANES)
                index = jnp.broadcast_to(mem[x, pl.ds(y, 1), span], (8, LANES))
                nodes[x, t, pl.ds(y, 8, stride=8), :] = pick(tables, index)
        values = []
        for i in range(3):
            value = 0.0
            for c in range(6):
                taken = jnp.concatenate(
                    [nodes[x, t, pl.ds(8 * c, 8), :] for t in range(NZ // LANES)], axis=1
                )
                value = value + ten[6 * i + c, x].astype(F32) * taken
            values.append(value)
        put_field(3, x, values)

    slabs(3, lift)

    def corrected(x):
        total = outside(3, x)
        put_field(
            4,
            x,
            [
                field[1, c, x + 1] + field[3, c, x + 1] - smoothing * total[c] * wgt[c, x]
                for c in range(3)
            ],
        )

    inside(3)
    wait_halo(3)
    slabs(4, corrected)

    inside(4)
    wait_halo(4)
    slabs(5, lambda x: put_field(5, x, smoothed(4, x)))

    def last(x):
        values = smoothed(5, x)
        for c in range(3):
            sol[c, x] = values[c]

    inside(5)
    wait_halo(5)
    slabs(None, last)

    for side in range(4):

        @pl.when(near[side][0])
        def _():
            for number in range(FIELDS):
                halo(number, side).wait_send()
            for number in range(2):
                coarse_halo(number, side ^ 1).wait_send()

    def sent_row(step, carry):
        to_row(step).wait_send()
        return carry

    lax.fori_loop(1, ny, sent_row, 0)

    def sent_part(step, carry):
        other = lax.rem(gy + step, ny)

        @pl.when(other_part(other))
        def _():
            to_part(other).wait_send()

        return carry

    lax.fori_loop(0, ny, sent_part, 0)


def body(nx, ny, rhs, stiffness, couplings, tentative, members, cst, ccp, col, snd, ctn, cmb, inv):
    couplings = couplings.reshape(63, FX, FY, NZ)
    tentative = tentative.reshape(18, FX, FY, NZ)
    cmb = cmb.reshape(1, A1)
    operands = (rhs, stiffness, couplings, tentative, members, cst, ccp, col, snd, ctn, cmb, inv)
    dma = pltpu.SemaphoreType.DMA
    scratch = [pltpu.VMEM(operand.shape, operand.dtype) for operand in operands]
    scratch += [
        pltpu.VMEM((3, FX, FY, NZ), F32),
        pltpu.VMEM((FIELDS, 3, FX + 2, FY, NZ), F32),
        pltpu.VMEM((FIELDS, 2, 3, FX, NZ), F32),
        pltpu.VMEM((FIELDS, 2, 3, FX, NZ), F32),
        pltpu.VMEM((3, FX, FY, NZ), F32),
        pltpu.VMEM((3, FX, FY, NZ), F32),
        pltpu.VMEM((FX, NZ // LANES, 8 * FY, LANES), F32),
        pltpu.VMEM((8, A1), F32),
        pltpu.VMEM((8, A1), F32),
        pltpu.VMEM((2, 8, A1 + 4 * H), F32),
        pltpu.VMEM((2, 4, 8, H), F32),
        pltpu.VMEM((40, A1), F32),
        pltpu.VMEM((1, 2 * LANES), F32),
        pltpu.VMEM((ny, 1, 2 * LANES), F32),
        pltpu.VMEM((1, 2 * LANES), F32),
        pltpu.VMEM((nx, 1, 2 * LANES), F32),
        dma((18,)),
        dma((FIELDS, 4)),
        dma((FIELDS, 4)),
        dma((2, 4)),
        dma((2, 4)),
        dma((ny,)),
        dma((ny,)),
        dma((ny,)),
        dma((nx,)),
    ]
    return pl.pallas_call(
        functools.partial(kernel, nx, ny),
        out_shape=(
            jax.ShapeDtypeStruct((3, FX, FY, NZ), F32),
            jax.ShapeDtypeStruct((6, A1), F32),
        ),
        in_specs=[pl.BlockSpec(memory_space=pl.ANY)] * len(operands),
        out_specs=(pl.BlockSpec(memory_space=pltpu.VMEM),) * 2,
        scratch_shapes=scratch,
        compiler_params=pltpu.CompilerParams(
            collective_id=0, has_side_effects=True, vmem_limit_bytes=60 * 1024 * 1024
        ),
    )(*operands)


def solution(mesh):
    placed = (
        P(None, "gx", "gy", None),
        P(None, "gx", "gy", None),
        P(None, None, None, "gx", "gy", None),
        P(None, None, "gx", "gy", None),
        P("gx", "gy", None),
        P(None, ("gx", "gy")),
        P(None, None, ("gx", "gy")),
        P(None, ("gx", "gy")),
        P(None, ("gx", "gy")),
        P(None, ("gx", "gy")),
        P(("gx", "gy")),
        P("gy", "gx"),
    )
    return jax.shard_map(
        functools.partial(body, mesh.shape["gx"], mesh.shape["gy"]),
        mesh=mesh,
        in_specs=placed,
        out_specs=(P(None, "gx", "gy", None), P(None, ("gx", "gy"))),
        check_vma=False,
    )
```

time: 847 us -> 77.1 us (0.09)
  local copies, waits for them, and re-layouts: 345 us -> 3.14 us
  other arithmetic: 243 us -> 0 us
  starting transfers between devices: 110 us -> 0 us
  blocking collectives: 105 us -> 0 us
  Pallas kernels: 0 us -> 72.2 us
  waiting for transfers between devices: 32.5 us -> 0 us
    gather x8 -> x0, local copies, waits for them, and re-layouts: 300 us -> none  [the longest x2 183 us: coarse_apply(): picked = jnp.take(extended, coarse_columns, axis=1)]
    scatter-add x2 -> x0, other arithmetic: 181 us -> none  [the longest x1 174 us: body(): jax.ops.segment_sum(contrib.reshape(6, -1).T, members.reshape(-1), num_se...]
    ppermute x32 -> x0, starting transfers between devices: 110 us -> none  [the longest x12 44.1 us: with_halo(): lax.ppermute(tail, axis, [(i, (i + 1) % count) for i in range(ends)])]
    unnamed x2 -> x0, blocking collectives: 77.5 us -> none
    pallas_call x0 -> x1, Pallas kernels: none -> 72.2 us  [body(): pl.pallas_call(functools.partial(kernel, nx, ny), out_shape=(jax.ShapeDty...]
    ppermute x32 -> x0, waiting for transfers between devices: 32.5 us -> none  [the longest x12 26.4 us: with_halo(): lax.ppermute(tail, axis, [(i, (i + 1) % count) for i in range(ends)])]
    psum x1 -> x0, blocking collectives: 27.8 us -> none  [body(): row_block = lax.psum(partial_value, 'gx')]
    transpose x2 -> x0, other arithmetic: 20.7 us -> none  [coarse_apply(): picked = jnp.transpose(picked, (1, 0, 2))]
  transfers between devices with their start and end apart: 32 -> 0, of which waited for: 14 -> 0; matrix products, arithmetic and copies ran while one was open for 0% -> 0% of each run, Pallas kernels for 0% -> 0%
where the time goes in v1:
time: 77.1 us; the launch traced here: 76 us
  Pallas kernels  72.2 us (94%)
  local copies, waits for them, and re-layouts  3.14 us (4%)
    pallas_call x1, Pallas kernels, body(): pl.pallas_call(functools.partial(kernel, nx, ny), out_shape=(jax.ShapeDty...  72.2 us
    unnamed x2, local copies, waits for them, and re-layouts  3.14 us

profile of v1, /device:TPU:9, one launch (start us, length us, event | category | flops | bytes accessed | tf_op | source)
XLA Modules:
  0.0 76.0 jit_solution(15434253677119825460)
XLA Ops:
  0.6 72.2 %shard_map.131 = (f32[3,8,8,512]{3,2,1,0:T(8,128)}, f32[6,1024]{1,0:T(8,128)}) custom-call(f32[3,8,8,512]{3,2,1,0:T(8,128)} %rhs_h.1, f32[3,8,8,512]{3,2,1,0:T(8,128)} %stf_h.1, bf16[63,8,8,512]{3,2,1,0:T(8,128)(2,1)} %bitcast.3, bf16[18,8,8,512]{3,2,1,0:T(8,128)(2,1)} %bitcast.4, s32[8,8,512]{2,1,0:T(8,128)} %mem_h.1, f32[6,1024]{1,0:T(8,128)} %cst_h.1, ...), custom_call_target="tpu_custom_call" | custom-call | tf_op jit(solution)/shard_map/pallas_call | solution.py:676
  72.9 1.8 %copy.16 = f32[3,8,8,512]{3,2,1,0:T(8,128)} copy(f32[3,8,8,512]{3,2,1,0:T(8,128)} %get-tuple-element.4) | data formatting | bytes 786432
  74.7 1.4 %copy.17 = f32[6,1024]{1,0:T(8,128)} copy(f32[6,1024]{1,0:T(8,128)} %get-tuple-element.5) | data formatting | bytes 49152

commit v2 on v1

--- a/solution.py
+++ b/solution.py
@@ -18,6 +18,8 @@
 A1 = 1024
 H = 256
 LANES = 128
+GROUP = 256
+WIDE = 2
 FIELDS = 6
 
 damping = 0.6
@@ -70,8 +72,8 @@
     ctn_h,
     cmb_h,
     inv_h,
-    sol,
-    csol,
+    sol_h,
+    csol_h,
     rhs,
     stf,
     cpl,
@@ -88,6 +90,10 @@
     field,
     yout,
     yin,
+    hout,
+    hin,
+    wout,
+    win,
     acc,
     resid,
     nodes,
@@ -96,11 +102,16 @@
     ext,
     cout,
     cacc,
+    sol,
+    csol,
+    ohm,
+    ohc,
     own_row,
     rows,
     part_row,
     parts,
     load_sem,
+    out_sem,
     fsend,
     frecv,
     csend,
@@ -119,15 +130,14 @@
     )
 
     loads = {}
-    pairs = [("rhs", rhs_h, rhs), ("stf", stf_h, stf)]
+    pairs = [("rhs", rhs_h, rhs), ("stf", stf_h, stf), ("mem", mem_h, mem)]
     for offset in (0, 5, 6, 1, 2, 3, 4):
         pairs.append(("cpl%d" % offset, cpl_h.at[pl.ds(9 * offset, 9)], cpl.at[pl.ds(9 * offset, 9)]))
     pairs += [
+        ("col", col_h, col),
         ("ten", ten_h, ten),
-        ("mem", mem_h, mem),
         ("cst", cst_h, cst),
         ("snd", snd_h, snd),
-        ("col", col_h, col),
         ("ccp", ccp_h, ccp),
         ("ctn", ctn_h, ctn),
         ("cmb", cmb_h, cmb),
@@ -162,16 +172,19 @@
 
     lax.fori_loop(0, nx, greet_sender, 0)
 
-    blank = jnp.zeros((FIELDS, 3, FY, NZ), F32)
+    def layer_out(number, side):
+        return wout.at[number, side] if number < WIDE else hout.at[number - WIDE, side]
+
+    def layer_in(number, side):
+        return win.at[number, side] if number < WIDE else hin.at[number - WIDE, side]
+
     for side, (there, _) in enumerate(near):
 
         @pl.when(jnp.logical_not(there))
         def _():
             for number in range(FIELDS):
-                if side < 2:
-                    field[number, :, 0 if side == 0 else FX + 1] = blank[0]
-                else:
-                    yin[number, side - 2] = blank[0]
+                target = layer_in(number, side)
+                target[...] = jnp.zeros(target.shape, target.dtype)
             for number in range(2):
                 ext[number, :, pl.ds(A1 + H * side, H)] = jnp.zeros((8, H), F32)
 
@@ -180,22 +193,22 @@
     part_row[...] = jnp.zeros_like(part_row)
 
     def halo(number, side):
-        if side == 0:
-            source, target, at = field.at[number, :, 1], field.at[number, :, FX + 1], 1
-        elif side == 1:
-            source, target, at = field.at[number, :, FX], field.at[number, :, 0], 0
-        elif side == 2:
-            source, target, at = yout.at[number, 0], yin.at[number, 1], 3
-        else:
-            source, target, at = yout.at[number, 1], yin.at[number, 0], 2
         return pltpu.make_async_remote_copy(
-            src_ref=source,
-            dst_ref=target,
+            src_ref=layer_out(number, side),
+            dst_ref=layer_in(number, side ^ 1),
             send_sem=fsend.at[number, side],
-            recv_sem=frecv.at[number, at],
+            recv_sem=frecv.at[number, side ^ 1],
             device_id=near[side][1],
             device_id_type=MESH,
         )
+
+    def pack(number, side, c, value):
+        target = layer_out(number, side)
+        target[c] = jnp.concatenate([value[:, : NZ // 2], value[:, NZ // 2 :]], axis=0).astype(target.dtype)
+
+    def received(number, side, j):
+        value = layer_in(number, side)[j].astype(F32)
+        return jnp.concatenate([value[:8], value[8:]], axis=1)
 
     def send_halo(number, side):
         @pl.when(near[side][0])
@@ -209,11 +222,19 @@
             def _():
                 halo(number, side ^ 1).wait_recv()
 
+        for side in range(2):
+            for j in range(3):
+                yin[side, j] = received(number, side + 2, j)
+
     def put_field(number, x, values):
         for c in range(3):
-            field[number, c, x + 1] = values[c]
-            yout[number, 0, c, pl.ds(x, 1), :] = values[c][0:1, :]
-            yout[number, 1, c, pl.ds(x, 1), :] = values[c][FY - 1 : FY, :]
+            field[number, c, x] = values[c]
+            yout[0, c, pl.ds(x, 1), :] = values[c][0:1, :]
+            yout[1, c, pl.ds(x, 1), :] = values[c][FY - 1 : FY, :]
+            if isinstance(x, int) and x == 0:
+                pack(number, 0, c, values[c])
+            if isinstance(x, int) and x == FX - 1:
+                pack(number, 1, c, values[c])
 
     def slabs(number, slab):
         slab(0)
@@ -229,8 +250,10 @@
 
         lax.fori_loop(1, FX - 1, inner, 0)
         if number is not None:
-            send_halo(number, 2)
-            send_halo(number, 3)
+            for side in range(2):
+                for c in range(3):
+                    pack(number, side + 2, c, yout[side, c])
+                send_halo(number, side + 2)
 
     def add(total, offset, x, j, view):
         for i in range(3):
@@ -240,16 +263,16 @@
         lane = lax.broadcasted_iota(jnp.int32, (FY, NZ), 1)
 
         def slab(x):
-            total = [stf[i, x] * field[number, i, x + 1] for i in range(3)]
+            total = [stf[i, x] * field[number, i, x] for i in range(3)]
             for j in range(3):
-                view = field[number, j, x + 1]
+                view = field[number, j, x]
                 add(total, 0, x, j, view)
                 add(total, 5, x, j, jnp.where(lane == 0, 0.0, pltpu.roll(view, 1, axis=1)))
                 add(total, 6, x, j, jnp.where(lane == NZ - 1, 0.0, pltpu.roll(view, NZ - 1, axis=1)))
                 if not (isinstance(x, int) and x == 0):
-                    add(total, 1, x, j, field[number, j, x])
+                    add(total, 1, x, j, field[number, j, x - 1])
                 if not (isinstance(x, int) and x == FX - 1):
-                    add(total, 2, x, j, field[number, j, x + 2])
+                    add(total, 2, x, j, field[number, j, x + 1])
             for i in range(3):
                 acc[i, x] = total[i]
 
@@ -259,15 +282,15 @@
         row = lax.broadcasted_iota(jnp.int32, (FY, NZ), 0)
         total = [acc[i, x] for i in range(3)]
         for j in range(3):
-            view = field[number, j, x + 1]
-            below = yin[number, 0, j, pl.ds(x, 1), :]
-            above = yin[number, 1, j, pl.ds(x, 1), :]
+            view = field[number, j, x]
+            below = yin[0, j, pl.ds(x, 1), :]
+            above = yin[1, j, pl.ds(x, 1), :]
             add(total, 3, x, j, jnp.where(row == 0, below, pltpu.roll(view, 1, axis=0)))
             add(total, 4, x, j, jnp.where(row == FY - 1, above, pltpu.roll(view, FY - 1, axis=0)))
             if isinstance(x, int) and x == 0:
-                add(total, 1, x, j, field[number, j, 0])
+                add(total, 1, x, j, received(number, 0, j))
             if isinstance(x, int) and x == FX - 1:
-                add(total, 2, x, j, field[number, j, FX + 1])
+                add(total, 2, x, j, received(number, 1, j))
         return total
 
     loads["rhs"].wait()
@@ -281,18 +304,55 @@
             values.append(damping * rhs[c, x] * weight)
         put_field(0, x, values)
 
-    def first_slab(x, carry):
-        first(x)
-        return carry
-
-    lax.fori_loop(0, FX, first_slab, 0)
-
     others = (
         sum(there.astype(jnp.int32) for there, _ in near) + (ny - 1) + nx - (gx == gy).astype(jnp.int32)
     )
     pl.semaphore_wait(barrier, others)
-    for side in range(4):
-        send_halo(0, side)
+    slabs(0, first)
+
+    count = lax.broadcasted_iota(jnp.int32, (16, NZ), 0).astype(F32).astype(BF16)
+
+    def one_hot(index):
+        width = index.shape[1]
+        low = jnp.broadcast_to(index & (LANES - 1), (16, width)).astype(F32).astype(BF16)
+        one, zero = jnp.ones((16, width), BF16), jnp.zeros((16, width), BF16)
+        return jnp.concatenate(
+            [jnp.where(low == count[:, :width] + float(16 * k), one, zero) for k in range(8)], axis=0
+        )
+
+    def hot_members(x, carry):
+        for y in range(FY):
+            ohm[x, :, pl.ds(NZ * y, NZ)] = one_hot(mem[x, pl.ds(y, 1), :])
+        return carry
+
+    def hot_columns(t, carry):
+        span = pl.ds(pl.multiple_of(GROUP * t, GROUP), GROUP)
+        columns = col[:, span]
+        for k in range(K):
+            ohc[k, :, span] = one_hot(columns[k : k + 1])
+        return carry
+
+    def choose(parts, index):
+        bit = LANES
+        while len(parts) > 1:
+            upper = (index & bit) != 0
+            parts = [jnp.where(upper, parts[at + 1], parts[at]) for at in range(0, len(parts), 2)]
+            bit *= 2
+        return parts[0]
+
+    def table(values):
+        pieces = [values[:, LANES * h : LANES * (h + 1)] for h in range(values.shape[1] // LANES)]
+        value = jnp.concatenate(pieces, axis=0)
+        rounded = value.astype(BF16).astype(F32)
+        return jnp.concatenate([rounded, value - rounded], axis=1).astype(BF16)
+
+    def look_up(entries, hot, index):
+        product = jnp.dot(entries, jnp.concatenate([hot, hot], axis=0), preferred_element_type=F32)
+        pieces = [product[8 * h : 8 * h + 8] for h in range(product.shape[0] // 8)]
+        return choose(pieces, jnp.broadcast_to(index, (8, index.shape[1])))
+
+    loads["mem"].wait()
+    lax.fori_loop(0, FX, hot_members, 0)
 
     for offset in (0, 5, 6, 1, 2, 3, 4):
         loads["cpl%d" % offset].wait()
@@ -300,7 +360,7 @@
     def smoothed(number, x):
         total = outside(number, x)
         return [
-            field[number, c, x + 1] + damping * (rhs[c, x] - total[c]) * wgt[c, x] for c in range(3)
+            field[number, c, x] + damping * (rhs[c, x] - total[c]) * wgt[c, x] for c in range(3)
         ]
 
     inside(0)
@@ -316,6 +376,8 @@
             values.append(left * wgt[c, x])
         put_field(2, x, values)
 
+    loads["col"].wait()
+    lax.fori_loop(0, A1 // GROUP, hot_columns, 0)
     inside(1)
     wait_halo(1)
     slabs(2, residual)
@@ -339,9 +401,6 @@
     wait_halo(2)
     slabs(None, restrict)
 
-    loads["mem"].wait()
-    count = lax.broadcasted_iota(jnp.int32, (16, NZ), 0).astype(F32).astype(BF16)
-
     def sums(x, total):
         for y in range(FY):
             value = jnp.concatenate(
@@ -350,14 +409,10 @@
             rounded = value.astype(BF16).astype(F32)
             both = jnp.concatenate([rounded, value - rounded], axis=0).astype(BF16)
             index = jnp.broadcast_to(mem[x, pl.ds(y, 1), :], (16, NZ))
-            low = (index & (LANES - 1)).astype(F32).astype(BF16)
             high = lax.shift_right_logical(index, 7).astype(F32).astype(BF16)
             zero = jnp.zeros((16, NZ), BF16)
-            one = jnp.ones((16, NZ), BF16)
             left = jnp.concatenate([jnp.where(high == float(h), both, zero) for h in range(8)], axis=0)
-            right = jnp.concatenate(
-                [jnp.where(low == count + float(16 * k), one, zero) for k in range(8)], axis=0
-            )
+            right = ohm[x, :, pl.ds(NZ * y, NZ)]
             total = total + lax.dot_general(
                 left, right, (((1,), (1,)), ((), ())), preferred_element_type=F32
             )
@@ -394,7 +449,7 @@
             def _():
                 coarse_halo(number, side).start()
 
-    sub = lax.broadcasted_iota(jnp.int32, (8, LANES), 0)
+    sub = lax.broadcasted_iota(jnp.int32, (8, GROUP), 0)
 
     def coarse_apply(number):
         for side in range(4):
@@ -403,13 +458,14 @@
             def _():
                 coarse_halo(number, side).wait_recv()
 
+        entries = table(ext[number])
+
         def group(t, carry):
-            span = pl.ds(pl.multiple_of(LANES * t, LANES), LANES)
-            tables = [ext[number, :, pl.ds(LANES * h, LANES)] for h in range((A1 + 4 * H) // LANES)]
-            total = [jnp.zeros((8 if piece < 4 else 4, LANES), F32) for piece in range(5)]
+            span = pl.ds(pl.multiple_of(GROUP * t, GROUP), GROUP)
+            total = [jnp.zeros((8 if piece < 4 else 4, GROUP), F32) for piece in range(5)]
             columns = col[:, span]
             for k in range(K):
-                base = pick(tables, jnp.broadcast_to(columns[k : k + 1], (8, LANES)))
+                base = look_up(entries, ohc[k, :, span], columns[k : k + 1])
                 up2, by4, down2 = (pltpu.roll(base, by, axis=0) for by in (6, 4, 2))
                 turned = (base, jnp.where(sub < 6, up2, by4), jnp.where(sub < 2, by4, down2))
                 for piece in range(5):
@@ -420,7 +476,7 @@
                 cacc[pl.ds(8 * piece, 8 if piece < 4 else 4), span] = total[piece]
             return carry
 
-        lax.fori_loop(0, A1 // LANES, group, 0)
+        lax.fori_loop(0, A1 // GROUP, group, 0)
 
     fold_row = lax.broadcasted_iota(jnp.int32, (8, 40), 0)
     fold_col = lax.broadcasted_iota(jnp.int32, (8, 40), 1)
@@ -431,7 +487,6 @@
         return jnp.dot(fold, cacc[...], precision=lax.Precision.HIGHEST, preferred_element_type=F32)
 
     send_coarse(0)
-    loads["col"].wait()
     loads["ccp"].wait()
     coarse_apply(0)
     s1 = crhs[...] - (cst8 * ext[0, :, pl.ds(0, A1)] + folded())
@@ -563,14 +618,16 @@
     solved = solved + damping * (crhs[...] - (cst8 * solved + folded())) / cst8
     y2[...] = solved
     csol[...] = solved[0:6]
+    csol_out = pltpu.make_async_copy(csol, csol_h, out_sem.at[FX])
+    csol_out.start()
+
+    entries = table(y2[...])
 
     def lift(x):
-        tables = [y2[:, pl.ds(LANES * h, LANES)] for h in range(A1 // LANES)]
         for y in range(FY):
+            taken = look_up(entries, ohm[x, :, pl.ds(NZ * y, NZ)], mem[x, pl.ds(y, 1), :])
             for t in range(NZ // LANES):
-                span = pl.ds(LANES * t, LANES)
-                index = jnp.broadcast_to(mem[x, pl.ds(y, 1), span], (8, LANES))
-                nodes[x, t, pl.ds(y, 8, stride=8), :] = pick(tables, index)
+                nodes[x, t, pl.ds(y, 8, stride=8), :] = taken[:, LANES * t : LANES * (t + 1)]
         values = []
         for i in range(3):
             value = 0.0
@@ -590,7 +647,7 @@
             4,
             x,
             [
-                field[1, c, x + 1] + field[3, c, x + 1] - smoothing * total[c] * wgt[c, x]
+                field[1, c, x] + field[3, c, x] - smoothing * total[c] * wgt[c, x]
                 for c in range(3)
             ],
         )
@@ -607,6 +664,10 @@
         values = smoothed(5, x)
         for c in range(3):
             sol[c, x] = values[c]
+        sol_out(x).start()
+
+    def sol_out(x):
+        return pltpu.make_async_copy(sol.at[:, x], sol_h.at[:, x], out_sem.at[x])
 
     inside(5)
     wait_halo(5)
@@ -637,6 +698,14 @@
         return carry
 
     lax.fori_loop(0, ny, sent_part, 0)
+    for x in range(FX):
+        sol_out(x).wait()
+    csol_out.wait()
+
+
+def write_out(sol, csol, sol_out, csol_out):
+    sol_out[...] = sol[...]
+    csol_out[...] = csol[...]
 
 
 def body(nx, ny, rhs, stiffness, couplings, tentative, members, cst, ccp, col, snd, ctn, cmb, inv):
@@ -648,9 +717,13 @@
     scratch = [pltpu.VMEM(operand.shape, operand.dtype) for operand in operands]
     scratch += [
         pltpu.VMEM((3, FX, FY, NZ), F32),
-        pltpu.VMEM((FIELDS, 3, FX + 2, FY, NZ), F32),
-        pltpu.VMEM((FIELDS, 2, 3, FX, NZ), F32),
-        pltpu.VMEM((FIELDS, 2, 3, FX, NZ), F32),
+        pltpu.VMEM((FIELDS, 3, FX, FY, NZ), F32),
+        pltpu.VMEM((2, 3, FX, NZ), F32),
+        pltpu.VMEM((2, 3, FX, NZ), F32),
+        pltpu.VMEM((FIELDS - WIDE, 4, 3, 16, NZ // 2), BF16),
+        pltpu.VMEM((FIELDS - WIDE, 4, 3, 16, NZ // 2), BF16),
+        pltpu.VMEM((WIDE, 4, 3, 16, NZ // 2), F32),
+        pltpu.VMEM((WIDE, 4, 3, 16, NZ // 2), F32),
         pltpu.VMEM((3, FX, FY, NZ), F32),
         pltpu.VMEM((3, FX, FY, NZ), F32),
         pltpu.VMEM((FX, NZ // LANES, 8 * FY, LANES), F32),
@@ -659,11 +732,16 @@
         pltpu.VMEM((2, 8, A1 + 4 * H), F32),
         pltpu.VMEM((2, 4, 8, H), F32),
         pltpu.VMEM((40, A1), F32),
+        pltpu.VMEM((3, FX, FY, NZ), F32),
+        pltpu.VMEM((6, A1), F32),
+        pltpu.VMEM((FX, LANES, FY * NZ), BF16),
+        pltpu.VMEM((K, LANES, A1), BF16),
         pltpu.VMEM((1, 2 * LANES), F32),
         pltpu.VMEM((ny, 1, 2 * LANES), F32),
         pltpu.VMEM((1, 2 * LANES), F32),
         pltpu.VMEM((nx, 1, 2 * LANES), F32),
         dma((18,)),
+        dma((FX + 1,)),
         dma((FIELDS, 4)),
         dma((FIELDS, 4)),
         dma((2, 4)),
@@ -673,19 +751,26 @@
         dma((ny,)),
         dma((nx,)),
     ]
-    return pl.pallas_call(
+    results = pl.pallas_call(
         functools.partial(kernel, nx, ny),
         out_shape=(
             jax.ShapeDtypeStruct((3, FX, FY, NZ), F32),
             jax.ShapeDtypeStruct((6, A1), F32),
         ),
         in_specs=[pl.BlockSpec(memory_space=pl.ANY)] * len(operands),
-        out_specs=(pl.BlockSpec(memory_space=pltpu.VMEM),) * 2,
+        out_specs=(pl.BlockSpec(memory_space=pl.ANY),) * 2,
         scratch_shapes=scratch,
         compiler_params=pltpu.CompilerParams(
-            collective_id=0, has_side_effects=True, vmem_limit_bytes=60 * 1024 * 1024
+            collective_id=0, has_side_effects=True, vmem_limit_bytes=56 * 1024 * 1024
         ),
     )(*operands)
+    return pl.pallas_call(
+        write_out,
+        out_shape=tuple(jax.ShapeDtypeStruct(result.shape, result.dtype) for result in results),
+        in_specs=[pl.BlockSpec(memory_space=pltpu.VMEM)] * 2,
+        out_specs=(pl.BlockSpec(memory_space=pltpu.VMEM),) * 2,
+        compiler_params=pltpu.CompilerParams(vmem_limit_bytes=60 * 1024 * 1024),
+    )(*results)
 
 
 def solution(mesh):

time: 77.1 us -> 69.6 us (0.903)
  Pallas kernels: 72.2 us -> 67.9 us
  local copies, waits for them, and re-layouts: 3.14 us -> 0 us
    pallas_call x1, Pallas kernels: 72.2 us -> 66.2 us  [body(): pl.pallas_call(functools.partial(kernel, nx, ny), out_shape=(jax.ShapeDty...]
    unnamed x2 -> x0, local copies, waits for them, and re-layouts: 3.14 us -> none
    pallas_call x0 -> x1, Pallas kernels: none -> 1.77 us  [body(): pl.pallas_call(write_out, out_shape=tuple((jax.ShapeDtypeStruct(result.sh...]
where the time goes in v2:
time: 69.6 us; the launch traced here: 68.6 us
  Pallas kernels  67.9 us (98%)
    pallas_call x1, Pallas kernels, body(): pl.pallas_call(functools.partial(kernel, nx, ny), out_shape=(jax.ShapeDty...  66.2 us
    pallas_call x1, Pallas kernels, body(): pl.pallas_call(write_out, out_shape=tuple((jax.ShapeDtypeStruct(result.sh...  1.77 us

profile of v2, /device:TPU:9, one launch (start us, length us, event | category | flops | bytes accessed | tf_op | source)
XLA Modules:
  0.0 68.6 jit_solution(15360533024800537251)
XLA Ops:
  0.6 66.2 %shard_map.131 = (f32[3,8,8,512]{3,2,1,0:T(8,128)}, f32[6,1024]{1,0:T(8,128)}) custom-call(f32[3,8,8,512]{3,2,1,0:T(8,128)} %rhs_h.1, f32[3,8,8,512]{3,2,1,0:T(8,128)} %stf_h.1, bf16[63,8,8,512]{3,2,1,0:T(8,128)(2,1)} %bitcast.3, bf16[18,8,8,512]{3,2,1,0:T(8,128)(2,1)} %bitcast.4, s32[8,8,512]{2,1,0:T(8,128)} %mem_h.1, f32[6,1024]{1,0:T(8,128)} %cst_h.1, ...), custom_call_target="tpu_custom_call" | custom-call | tf_op jit(solution)/shard_map/pallas_call | solution.py:754
  66.8 1.8 %shard_map.132 = (f32[3,8,8,512]{3,2,1,0:T(8,128)}, f32[6,1024]{1,0:T(8,128)}) custom-call(f32[3,8,8,512]{3,2,1,0:T(8,128)} %get-tuple-element.4.sol, f32[6,1024]{1,0:T(8,128)} %get-tuple-element.5.csol), custom_call_target="tpu_custom_call" | custom-call | tf_op jit(solution)/shard_map/pallas_call | solution.py:767

commit v3 on v2

--- a/solution.py
+++ b/solution.py
@@ -18,7 +18,8 @@
 A1 = 1024
 H = 256
 LANES = 128
-GROUP = 256
+GROUP = 512
+HALF = 256
 WIDE = 2
 FIELDS = 6
 
@@ -102,6 +103,7 @@
     ext,
     cout,
     cacc,
+    invs,
     sol,
     csol,
     ohm,
@@ -110,6 +112,7 @@
     rows,
     part_row,
     parts,
+    wave,
     load_sem,
     out_sem,
     fsend,
@@ -129,6 +132,28 @@
         (gy < ny - 1, {"gx": gx, "gy": jnp.minimum(gy + 1, ny - 1)}),
     )
 
+    barrier = pltpu.get_barrier_semaphore()
+
+    def tell(semaphore, steps):
+        for device in (
+            {"gx": lax.rem(gx + nx - steps, nx), "gy": gy},
+            {"gx": lax.rem(gx + steps, nx), "gy": gy},
+            {"gx": gx, "gy": lax.rem(gy + ny - steps, ny)},
+            {"gx": gx, "gy": lax.rem(gy + steps, ny)},
+        ):
+            pl.semaphore_signal(semaphore, inc=1, device_id=device, device_id_type=MESH)
+
+    def announce(number):
+        if 2 << number < nx:
+            tell(wave.at[number], 1 << number)
+
+    def heard(number):
+        if 2 << number < nx:
+            pl.semaphore_wait(wave.at[number], 4)
+
+    if nx > 1:
+        tell(barrier, 1)
+
     loads = {}
     pairs = [("rhs", rhs_h, rhs), ("stf", stf_h, stf), ("mem", mem_h, mem)]
     for offset in (0, 5, 6, 1, 2, 3, 4):
@@ -147,31 +172,6 @@
         loads[name] = pltpu.make_async_copy(source, target, load_sem.at[number])
         loads[name].start()
 
-    barrier = pltpu.get_barrier_semaphore()
-    for there, device in near:
-
-        @pl.when(there)
-        def _():
-            pl.semaphore_signal(barrier, inc=1, device_id=device, device_id_type=MESH)
-
-    def greet(step, carry):
-        other = lax.rem(gy + step, ny)
-        pl.semaphore_signal(barrier, inc=1, device_id={"gx": gx, "gy": other}, device_id_type=MESH)
-        return carry
-
-    lax.fori_loop(1, ny, greet, 0)
-
-    def greet_sender(step, carry):
-        other = lax.rem(gx + step, nx)
-
-        @pl.when(jnp.logical_not(jnp.logical_and(other == gx, gx == gy)))
-        def _():
-            pl.semaphore_signal(barrier, inc=1, device_id={"gx": other, "gy": gx}, device_id_type=MESH)
-
-        return carry
-
-    lax.fori_loop(0, nx, greet_sender, 0)
-
     def layer_out(number, side):
         return wout.at[number, side] if number < WIDE else hout.at[number - WIDE, side]
 
@@ -304,10 +304,9 @@
             values.append(damping * rhs[c, x] * weight)
         put_field(0, x, values)
 
-    others = (
-        sum(there.astype(jnp.int32) for there, _ in near) + (ny - 1) + nx - (gx == gy).astype(jnp.int32)
-    )
-    pl.semaphore_wait(barrier, others)
+    if nx > 1:
+        pl.semaphore_wait(barrier, 4)
+    announce(0)
     slabs(0, first)
 
     count = lax.broadcasted_iota(jnp.int32, (16, NZ), 0).astype(F32).astype(BF16)
@@ -364,6 +363,8 @@
         ]
 
     inside(0)
+    heard(0)
+    announce(1)
     wait_halo(0)
     slabs(1, lambda x: put_field(1, x, smoothed(0, x)))
 
@@ -376,9 +377,9 @@
             values.append(left * wgt[c, x])
         put_field(2, x, values)
 
-    loads["col"].wait()
-    lax.fori_loop(0, A1 // GROUP, hot_columns, 0)
     inside(1)
+    heard(1)
+    announce(2)
     wait_halo(1)
     slabs(2, residual)
 
@@ -397,7 +398,13 @@
                 if c < 2:
                     nodes[x, t, pl.ds(8 * (c + 6), 8), :] = part
 
+    loads["inv"].wait()
+    whole = inv[...]
+    rounded = whole.astype(BF16)
+    invs[0] = rounded
+    invs[1] = (whole - rounded.astype(F32)).astype(BF16)
     inside(2)
+    heard(2)
     wait_halo(2)
     slabs(None, restrict)
 
@@ -487,13 +494,14 @@
         return jnp.dot(fold, cacc[...], precision=lax.Precision.HIGHEST, preferred_element_type=F32)
 
     send_coarse(0)
+    loads["col"].wait()
+    lax.fori_loop(0, A1 // GROUP, hot_columns, 0)
     loads["ccp"].wait()
     coarse_apply(0)
     s1 = crhs[...] - (cst8 * ext[0, :, pl.ds(0, A1)] + folded())
 
     loads["ctn"].wait()
     loads["cmb"].wait()
-    loads["inv"].wait()
     lane = lax.broadcasted_iota(jnp.int32, (1, 2 * LANES), 1)
     upper = cmb[...] != 0
     row = jnp.zeros((1, 2 * LANES), F32)
@@ -531,25 +539,23 @@
             device_id_type=MESH,
         )
 
-    def send_row(step, carry):
+    for step in range(1, ny):
         to_row(step).start()
-        return carry
-
-    lax.fori_loop(1, ny, send_row, 0)
-
-    def take_row(step, carry):
+    for step in range(1, ny):
         from_row(lax.rem(gy + step, ny)).wait_recv()
-        return carry
-
-    lax.fori_loop(1, ny, take_row, 0)
     rows[gy] = row
     entries = jnp.sum(rows[...], axis=0)
     block = inv.shape[1]
-    values = jnp.broadcast_to(entries[:, :block], (8, block))
-    product = lax.dot_general(
-        values, inv[...], (((1,), (1,)), ((), ())), precision=lax.Precision.HIGHEST, preferred_element_type=F32
+    values = entries[:, :block]
+    rounded = values.astype(BF16).astype(F32)
+    values = jnp.concatenate(
+        [jnp.broadcast_to(rounded, (8, block)), jnp.broadcast_to(values - rounded, (8, block))], axis=0
+    ).astype(BF16)
+    upper_part, lower_part = (
+        lax.dot_general(values, invs[at], (((1,), (1,)), ((), ())), preferred_element_type=F32) for at in range(2)
     )
-    part_row[:, pl.ds(0, block)] = product[0:1]
+    product = upper_part[0:1] + (upper_part[8:9] + lower_part[0:1] + lower_part[8:9])
+    part_row[:, pl.ds(0, block)] = product
 
     def to_part(other):
         return pltpu.make_async_remote_copy(
@@ -571,34 +577,23 @@
             device_id_type=MESH,
         )
 
-    def other_part(other):
-        return jnp.logical_not(jnp.logical_and(other == gy, gx == gy))
-
-    def send_part(step, carry):
-        other = lax.rem(gy + step, ny)
-
-        @pl.when(other_part(other))
-        def _():
-            to_part(other).start()
-
-        return carry
-
-    lax.fori_loop(0, ny, send_part, 0)
-
-    def take_part(step, carry):
-        other = lax.rem(gx + step, nx)
-
-        @pl.when(jnp.logical_not(jnp.logical_and(other == gx, gx == gy)))
-        def _():
-            from_part(other).wait_recv()
-
-        return carry
-
-    lax.fori_loop(0, nx, take_part, 0)
+    for step in range(1, ny):
+        to_part(lax.rem(gy + step, ny)).start()
+
+    @pl.when(gx != gy)
+    def _():
+        to_part(gy).start()
 
     @pl.when(gx == gy)
     def _():
         parts[gx] = part_row[...]
+
+    for step in range(1, nx):
+        from_part(lax.rem(gx + step, nx)).wait_recv()
+
+    @pl.when(gx != gy)
+    def _():
+        from_part(gx).wait_recv()
 
     coarsest = jnp.sum(parts[...], axis=0)
 
@@ -622,12 +617,18 @@
     csol_out.start()
 
     entries = table(y2[...])
+    tables = [y2[:, pl.ds(LANES * h, LANES)] for h in range(A1 // LANES)]
 
     def lift(x):
         for y in range(FY):
-            taken = look_up(entries, ohm[x, :, pl.ds(NZ * y, NZ)], mem[x, pl.ds(y, 1), :])
+            taken = look_up(entries, ohm[x, :, pl.ds(NZ * y, HALF)], mem[x, pl.ds(y, 1), pl.ds(0, HALF)])
             for t in range(NZ // LANES):
-                nodes[x, t, pl.ds(y, 8, stride=8), :] = taken[:, LANES * t : LANES * (t + 1)]
+                if t < HALF // LANES:
+                    value = taken[:, LANES * t : LANES * (t + 1)]
+                else:
+                    index = mem[x, pl.ds(y, 1), pl.ds(LANES * t, LANES)]
+                    value = pick(tables, jnp.broadcast_to(index, (8, LANES)))
+                nodes[x, t, pl.ds(y, 8, stride=8), :] = value
         values = []
         for i in range(3):
             value = 0.0
@@ -682,22 +683,14 @@
             for number in range(2):
                 coarse_halo(number, side ^ 1).wait_send()
 
-    def sent_row(step, carry):
+    for step in range(1, ny):
         to_row(step).wait_send()
-        return carry
-
-    lax.fori_loop(1, ny, sent_row, 0)
-
-    def sent_part(step, carry):
-        other = lax.rem(gy + step, ny)
-
-        @pl.when(other_part(other))
-        def _():
-            to_part(other).wait_send()
-
-        return carry
-
-    lax.fori_loop(0, ny, sent_part, 0)
+        to_part(lax.rem(gy + step, ny)).wait_send()
+
+    @pl.when(gx != gy)
+    def _():
+        to_part(gy).wait_send()
+
     for x in range(FX):
         sol_out(x).wait()
     csol_out.wait()
@@ -732,6 +725,7 @@
         pltpu.VMEM((2, 8, A1 + 4 * H), F32),
         pltpu.VMEM((2, 4, 8, H), F32),
         pltpu.VMEM((40, A1), F32),
+        pltpu.VMEM((2, *inv.shape), BF16),
         pltpu.VMEM((3, FX, FY, NZ), F32),
         pltpu.VMEM((6, A1), F32),
         pltpu.VMEM((FX, LANES, FY * NZ), BF16),
@@ -740,6 +734,7 @@
         pltpu.VMEM((ny, 1, 2 * LANES), F32),
         pltpu.VMEM((1, 2 * LANES), F32),
         pltpu.VMEM((nx, 1, 2 * LANES), F32),
+        pltpu.SemaphoreType.REGULAR((3,)),
         dma((18,)),
         dma((FX + 1,)),
         dma((FIELDS, 4)),

time: 69.6 us -> 64.7 us (0.930)
  Pallas kernels: 67.9 us -> 63.3 us
    pallas_call x1, Pallas kernels: 66.2 us -> 61.5 us  [body(): pl.pallas_call(functools.partial(kernel, nx, ny), out_shape=(jax.ShapeDty...]
where the time goes in v3:
time: 64.7 us; the launch traced here: 63.9 us
  Pallas kernels  63.3 us (98%)
    pallas_call x1, Pallas kernels, body(): pl.pallas_call(functools.partial(kernel, nx, ny), out_shape=(jax.ShapeDty...  61.5 us
    pallas_call x1, Pallas kernels, body(): pl.pallas_call(write_out, out_shape=tuple((jax.ShapeDtypeStruct(result.sh...  1.77 us

profile of v3, /device:TPU:9, one launch (start us, length us, event | category | flops | bytes accessed | tf_op | source)
XLA Modules:
  0.0 63.9 jit_solution(1784711162600801237)
XLA Ops:
  0.6 61.5 %shard_map.131 = (f32[3,8,8,512]{3,2,1,0:T(8,128)}, f32[6,1024]{1,0:T(8,128)}) custom-call(f32[3,8,8,512]{3,2,1,0:T(8,128)} %rhs_h.1, f32[3,8,8,512]{3,2,1,0:T(8,128)} %stf_h.1, bf16[63,8,8,512]{3,2,1,0:T(8,128)(2,1)} %bitcast.3, bf16[18,8,8,512]{3,2,1,0:T(8,128)(2,1)} %bitcast.4, s32[8,8,512]{2,1,0:T(8,128)} %mem_h.1, f32[6,1024]{1,0:T(8,128)} %cst_h.1, ...), custom_call_target="tpu_custom_call" | custom-call | tf_op jit(solution)/shard_map/pallas_call | solution.py:749
  62.1 1.8 %shard_map.132 = (f32[3,8,8,512]{3,2,1,0:T(8,128)}, f32[6,1024]{1,0:T(8,128)}) custom-call(f32[3,8,8,512]{3,2,1,0:T(8,128)} %get-tuple-element.4.sol, f32[6,1024]{1,0:T(8,128)} %get-tuple-element.5.csol), custom_call_target="tpu_custom_call" | custom-call | tf_op jit(solution)/shard_map/pallas_call | solution.py:762

commit v4 on v3

--- a/solution.py
+++ b/solution.py
@@ -103,6 +103,8 @@
     ext,
     cout,
     cacc,
+    lift1,
+    lout,
     invs,
     sol,
     csol,
@@ -159,13 +161,13 @@
     for offset in (0, 5, 6, 1, 2, 3, 4):
         pairs.append(("cpl%d" % offset, cpl_h.at[pl.ds(9 * offset, 9)], cpl.at[pl.ds(9 * offset, 9)]))
     pairs += [
+        ("snd", snd_h, snd),
+        ("ctn", ctn_h, ctn),
+        ("cmb", cmb_h, cmb),
         ("col", col_h, col),
         ("ten", ten_h, ten),
         ("cst", cst_h, cst),
-        ("snd", snd_h, snd),
         ("ccp", ccp_h, ccp),
-        ("ctn", ctn_h, ctn),
-        ("cmb", cmb_h, cmb),
         ("inv", inv_h, inv),
     ]
     for number, (name, source, target) in enumerate(pairs):
@@ -185,10 +187,12 @@
             for number in range(FIELDS):
                 target = layer_in(number, side)
                 target[...] = jnp.zeros(target.shape, target.dtype)
-            for number in range(2):
-                ext[number, :, pl.ds(A1 + H * side, H)] = jnp.zeros((8, H), F32)
-
-    cacc[pl.ds(32, 8), :] = jnp.zeros((8, A1), F32)
+            ext[0, :, pl.ds(A1 + H * side, H)] = jnp.zeros((8, H), F32)
+            lift1[:, pl.ds(A1 + H * side, H)] = jnp.zeros((40, H), F32)
+            if side < 2:
+                parts[2 * side] = jnp.zeros(parts.shape[1:], F32)
+
+    cacc[pl.ds(32, 8), :] = jnp.zeros((8, A1 + 4 * H), F32)
     own_row[...] = jnp.zeros_like(own_row)
     part_row[...] = jnp.zeros_like(part_row)
 
@@ -293,6 +297,45 @@
                 add(total, 2, x, j, received(number, 1, j))
         return total
 
+    def coarse_halo(number, side):
+        span = pl.ds(A1 + H * side, H)
+        return pltpu.make_async_remote_copy(
+            src_ref=lout.at[side] if number else cout.at[side],
+            dst_ref=lift1.at[:, span] if number else ext.at[0, :, span],
+            send_sem=csend.at[number, side],
+            recv_sem=crecv.at[number, side],
+            device_id=near[side ^ 1][1],
+            device_id_type=MESH,
+        )
+
+    def wait_coarse(number):
+        for side in range(4):
+
+            @pl.when(near[side][0])
+            def _():
+                coarse_halo(number, side).wait_recv()
+
+    def send_lift():
+        lift1[pl.ds(0, 32), pl.ds(0, A1)] = ctn[pl.ds(0, 32), :]
+        members = jnp.broadcast_to(cmb[...].astype(F32), (4, A1))
+        lift1[pl.ds(32, 8), pl.ds(0, A1)] = jnp.concatenate([ctn[pl.ds(32, 4), :], members], axis=0)
+
+        def one(piece, carry):
+            rows8 = pl.ds(pl.multiple_of(8 * piece, 8), 8)
+            tables = [lift1[rows8, pl.ds(LANES * h, LANES)] for h in range(A1 // LANES)]
+            for side in range(4):
+                for t in range(H // LANES):
+                    span = pl.ds(LANES * t, LANES)
+                    lout[side, rows8, span] = pick(tables, jnp.broadcast_to(snd[side : side + 1, span], (8, LANES)))
+            return carry
+
+        lax.fori_loop(0, 5, one, 0)
+        for side in range(4):
+
+            @pl.when(near[side ^ 1][0])
+            def _():
+                coarse_halo(1, side).start()
+
     loads["rhs"].wait()
     loads["stf"].wait()
 
@@ -377,6 +420,10 @@
             values.append(left * wgt[c, x])
         put_field(2, x, values)
 
+    loads["snd"].wait()
+    loads["ctn"].wait()
+    loads["cmb"].wait()
+    send_lift()
     inside(1)
     heard(1)
     announce(2)
@@ -406,6 +453,7 @@
     inside(2)
     heard(2)
     wait_halo(2)
+    wait_coarse(1)
     slabs(None, restrict)
 
     def sums(x, total):
@@ -428,43 +476,26 @@
     gathered = lax.fori_loop(0, FX, sums, jnp.zeros((LANES, LANES), F32))
 
     loads["cst"].wait()
-    loads["snd"].wait()
     for h in range(8):
         span = pl.ds(LANES * h, LANES)
         crhs[:, span] = gathered[16 * h : 16 * h + 8] + gathered[16 * h + 8 : 16 * h + 16]
     cst8 = jnp.concatenate([cst[...], cst[0:2, :]], axis=0)
     ext[0, :, pl.ds(0, A1)] = damping * crhs[...] / cst8
 
-    def coarse_halo(number, side):
-        return pltpu.make_async_remote_copy(
-            src_ref=cout.at[number, side],
-            dst_ref=ext.at[number, :, pl.ds(A1 + H * side, H)],
-            send_sem=csend.at[number, side],
-            recv_sem=crecv.at[number, side],
-            device_id=near[side ^ 1][1],
-            device_id_type=MESH,
-        )
-
-    def send_coarse(number):
-        tables = [ext[number, :, pl.ds(LANES * h, LANES)] for h in range(A1 // LANES)]
+    def send_coarse():
+        tables = [ext[0, :, pl.ds(LANES * h, LANES)] for h in range(A1 // LANES)]
         for side in range(4):
             for t in range(H // LANES):
                 index = jnp.broadcast_to(snd[side : side + 1, pl.ds(LANES * t, LANES)], (8, LANES))
-                cout[number, side, :, pl.ds(LANES * t, LANES)] = pick(tables, index)
+                cout[side, :, pl.ds(LANES * t, LANES)] = pick(tables, index)
 
             @pl.when(near[side ^ 1][0])
             def _():
-                coarse_halo(number, side).start()
+                coarse_halo(0, side).start()
 
     sub = lax.broadcasted_iota(jnp.int32, (8, GROUP), 0)
 
     def coarse_apply(number):
-        for side in range(4):
-
-            @pl.when(near[side][0])
-            def _():
-                coarse_halo(number, side).wait_recv()
-
         entries = table(ext[number])
 
         def group(t, carry):
@@ -491,17 +522,16 @@
     fold = jnp.logical_and(fold_col >= 6 * fold_row, fold_col < 6 * fold_row + 6).astype(F32)
 
     def folded():
-        return jnp.dot(fold, cacc[...], precision=lax.Precision.HIGHEST, preferred_element_type=F32)
-
-    send_coarse(0)
+        return jnp.dot(fold, cacc[:, pl.ds(0, A1)], precision=lax.Precision.HIGHEST, preferred_element_type=F32)
+
+    send_coarse()
     loads["col"].wait()
     lax.fori_loop(0, A1 // GROUP, hot_columns, 0)
     loads["ccp"].wait()
+    wait_coarse(0)
     coarse_apply(0)
     s1 = crhs[...] - (cst8 * ext[0, :, pl.ds(0, A1)] + folded())
 
-    loads["ctn"].wait()
-    loads["cmb"].wait()
     lane = lax.broadcasted_iota(jnp.int32, (1, 2 * LANES), 1)
     upper = cmb[...] != 0
     row = jnp.zeros((1, 2 * LANES), F32)
@@ -557,57 +587,74 @@
     product = upper_part[0:1] + (upper_part[8:9] + lower_part[0:1] + lower_part[8:9])
     part_row[:, pl.ds(0, block)] = product
 
-    def to_part(other):
+    def part(at, row_of, semaphore, device):
         return pltpu.make_async_remote_copy(
             src_ref=part_row,
-            dst_ref=parts.at[gx],
-            send_sem=psend.at[other],
-            recv_sem=precv.at[gx],
-            device_id={"gx": gy, "gy": other},
+            dst_ref=parts.at[at, row_of],
+            send_sem=psend.at[at, semaphore],
+            recv_sem=precv.at[at, row_of],
+            device_id=device,
             device_id_type=MESH,
         )
 
-    def from_part(other):
-        return pltpu.make_async_remote_copy(
-            src_ref=part_row,
-            dst_ref=parts.at[other],
-            send_sem=psend.at[other],
-            recv_sem=precv.at[other],
-            device_id={"gx": other, "gy": gx},
-            device_id_type=MESH,
-        )
-
-    for step in range(1, ny):
-        to_part(lax.rem(gy + step, ny)).start()
-
-    @pl.when(gx != gy)
-    def _():
-        to_part(gy).start()
-
-    @pl.when(gx == gy)
-    def _():
-        parts[gx] = part_row[...]
-
-    for step in range(1, nx):
-        from_part(lax.rem(gx + step, nx)).wait_recv()
-
-    @pl.when(gx != gy)
-    def _():
-        from_part(gx).wait_recv()
-
-    coarsest = jnp.sum(parts[...], axis=0)
-
-    for piece in range(5):
-        size = 8 if piece < 4 else 4
-        at = pl.ds(8 * piece, size)
-        _, c = rows_of(piece, size)
-        spread = [
-            jnp.sum(jnp.where(lane == 12 * gy + 2 * c + a, coarsest, 0.0), axis=1, keepdims=True)
-            for a in range(2)
-        ]
-        cacc[at, :] = ctn[at, :] * jnp.where(upper, spread[1], spread[0])
-    ext[1, :, pl.ds(0, A1)] = ext[0, :, pl.ds(0, A1)] + folded()
-    send_coarse(1)
+    def to_part(at, step):
+        other = lax.rem(gy + step, ny)
+        return part(at, gx, step, {"gx": jnp.clip(gy + 1 - at, 0, nx - 1), "gy": other})
+
+    def from_part(at, step):
+        other = lax.rem(gx + step, nx)
+        return part(at, other, 0, {"gx": other, "gy": jnp.clip(gx + at - 1, 0, ny - 1)})
+
+    for at in (1, 0, 2):
+        target, held = gy + 1 - at, gx + at - 1
+
+        @pl.when(jnp.logical_and(target >= 0, target < nx))
+        def _():
+            for step in range(1, ny):
+                to_part(at, step).start()
+
+            @pl.when(gx != target)
+            def _():
+                to_part(at, 0).start()
+
+            @pl.when(gx == target)
+            def _():
+                parts[at, gx] = part_row[...]
+
+    for at in (1, 0, 2):
+        target, held = gy + 1 - at, gx + at - 1
+
+        @pl.when(jnp.logical_and(held >= 0, held < ny))
+        def _():
+            for step in range(1, nx):
+                from_part(at, step).wait_recv()
+
+            @pl.when(gy != held)
+            def _():
+                from_part(at, 0).wait_recv()
+
+    coarsest = [jnp.sum(parts[at], axis=0) for at in range(3)]
+
+    places = (
+        (0, A1, 1, gy),
+        (A1, H, 0, gy),
+        (A1 + H, H, 2, gy),
+        (A1 + 2 * H, H, 1, gy - 1),
+        (A1 + 3 * H, H, 1, gy + 1),
+    )
+    for start, length, at, owner in places:
+        span = pl.ds(start, length)
+        one = lift1[36:37, span] != 0.0
+        for piece in range(5):
+            size = 8 if piece < 4 else 4
+            _, c = rows_of(piece, size)
+            spread = [
+                jnp.sum(jnp.where(lane == 12 * owner + 2 * c + a, coarsest[at], 0.0), axis=1, keepdims=True)
+                for a in range(2)
+            ]
+            here = pl.ds(8 * piece, size)
+            cacc[here, span] = lift1[here, span] * jnp.where(one, spread[1], spread[0])
+    ext[1] = ext[0] + jnp.dot(fold, cacc[...], precision=lax.Precision.HIGHEST, preferred_element_type=F32)
     coarse_apply(1)
     solved = ext[1, :, pl.ds(0, A1)]
     solved = solved + damping * (crhs[...] - (cst8 * solved + folded())) / cst8
@@ -685,11 +732,17 @@
 
     for step in range(1, ny):
         to_row(step).wait_send()
-        to_part(lax.rem(gy + step, ny)).wait_send()
-
-    @pl.when(gx != gy)
-    def _():
-        to_part(gy).wait_send()
+    for at in range(3):
+        target = gy + 1 - at
+
+        @pl.when(jnp.logical_and(target >= 0, target < nx))
+        def _():
+            for step in range(1, ny):
+                to_part(at, step).wait_send()
+
+            @pl.when(gx != target)
+            def _():
+                to_part(at, 0).wait_send()
 
     for x in range(FX):
         sol_out(x).wait()
@@ -723,8 +776,10 @@
         pltpu.VMEM((8, A1), F32),
         pltpu.VMEM((8, A1), F32),
         pltpu.VMEM((2, 8, A1 + 4 * H), F32),
-        pltpu.VMEM((2, 4, 8, H), F32),
-        pltpu.VMEM((40, A1), F32),
+        pltpu.VMEM((4, 8, H), F32),
+        pltpu.VMEM((40, A1 + 4 * H), F32),
+        pltpu.VMEM((40, A1 + 4 * H), F32),
+        pltpu.VMEM((4, 40, H), F32),
         pltpu.VMEM((2, *inv.shape), BF16),
         pltpu.VMEM((3, FX, FY, NZ), F32),
         pltpu.VMEM((6, A1), F32),
@@ -733,7 +788,7 @@
         pltpu.VMEM((1, 2 * LANES), F32),
         pltpu.VMEM((ny, 1, 2 * LANES), F32),
         pltpu.VMEM((1, 2 * LANES), F32),
-        pltpu.VMEM((nx, 1, 2 * LANES), F32),
+        pltpu.VMEM((3, nx, 1, 2 * LANES), F32),
         pltpu.SemaphoreType.REGULAR((3,)),
         dma((18,)),
         dma((FX + 1,)),
@@ -743,8 +798,8 @@
         dma((2, 4)),
         dma((ny,)),
         dma((ny,)),
-        dma((ny,)),
-        dma((nx,)),
+        dma((3, ny)),
+        dma((3, nx)),
     ]
     results = pl.pallas_call(
         functools.partial(kernel, nx, ny),

time: 64.7 us -> 62.9 us (0.972); the launches traced: 63.9 us -> 62.8 us
  Pallas kernels: 63.3 us -> 62.2 us
    pallas_call x1, Pallas kernels: 61.5 us -> 60.4 us  [body(): pl.pallas_call(functools.partial(kernel, nx, ny), out_shape=(jax.ShapeDty...]
where the time goes in v4:
time: 62.9 us; the launch traced here: 62.8 us
  Pallas kernels  62.2 us (99%)
  between operations  0.64 us (1%)
    pallas_call x1, Pallas kernels, body(): pl.pallas_call(functools.partial(kernel, nx, ny), out_shape=(jax.ShapeDty...  60.4 us
    pallas_call x1, Pallas kernels, body(): pl.pallas_call(write_out, out_shape=tuple((jax.ShapeDtypeStruct(result.sh...  1.77 us

profile of v4, /device:TPU:9, one launch (start us, length us, event | category | flops | bytes accessed | tf_op | source)
XLA Modules:
  0.0 62.8 jit_solution(2146384478777866579)
XLA Ops:
  0.6 60.4 %shard_map.131 = (f32[3,8,8,512]{3,2,1,0:T(8,128)}, f32[6,1024]{1,0:T(8,128)}) custom-call(f32[3,8,8,512]{3,2,1,0:T(8,128)} %rhs_h.1, f32[3,8,8,512]{3,2,1,0:T(8,128)} %stf_h.1, bf16[63,8,8,512]{3,2,1,0:T(8,128)(2,1)} %bitcast.3, bf16[18,8,8,512]{3,2,1,0:T(8,128)(2,1)} %bitcast.4, s32[8,8,512]{2,1,0:T(8,128)} %mem_h.1, f32[6,1024]{1,0:T(8,128)} %cst_h.1, ...), custom_call_target="tpu_custom_call" | custom-call | tf_op jit(solution)/shard_map/pallas_call | solution.py:804
  61.0 1.8 %shard_map.132 = (f32[3,8,8,512]{3,2,1,0:T(8,128)}, f32[6,1024]{1,0:T(8,128)}) custom-call(f32[3,8,8,512]{3,2,1,0:T(8,128)} %get-tuple-element.4.sol, f32[6,1024]{1,0:T(8,128)} %get-tuple-element.5.csol), custom_call_target="tpu_custom_call" | custom-call | tf_op jit(solution)/shard_map/pallas_call | solution.py:817

commit v5 on v4

--- a/solution.py
+++ b/solution.py
@@ -73,8 +73,8 @@
     ctn_h,
     cmb_h,
     inv_h,
-    sol_h,
-    csol_h,
+    sol,
+    csol,
     rhs,
     stf,
     cpl,
@@ -106,8 +106,6 @@
     lift1,
     lout,
     invs,
-    sol,
-    csol,
     ohm,
     ohc,
     own_row,
@@ -116,7 +114,6 @@
     parts,
     wave,
     load_sem,
-    out_sem,
     fsend,
     frecv,
     csend,
@@ -521,8 +518,15 @@
     fold_row = jnp.where(fold_row < 6, fold_row, fold_row - 6)
     fold = jnp.logical_and(fold_col >= 6 * fold_row, fold_col < 6 * fold_row + 6).astype(F32)
 
+    fold = fold.astype(BF16)
+
+    def fold_rows(values):
+        rounded = values.astype(BF16)
+        rest = (values - rounded.astype(F32)).astype(BF16)
+        return jnp.dot(fold, rounded, preferred_element_type=F32) + jnp.dot(fold, rest, preferred_element_type=F32)
+
     def folded():
-        return jnp.dot(fold, cacc[:, pl.ds(0, A1)], precision=lax.Precision.HIGHEST, preferred_element_type=F32)
+        return fold_rows(cacc[:, pl.ds(0, A1)])
 
     send_coarse()
     loads["col"].wait()
@@ -654,14 +658,12 @@
             ]
             here = pl.ds(8 * piece, size)
             cacc[here, span] = lift1[here, span] * jnp.where(one, spread[1], spread[0])
-    ext[1] = ext[0] + jnp.dot(fold, cacc[...], precision=lax.Precision.HIGHEST, preferred_element_type=F32)
+    ext[1] = ext[0] + fold_rows(cacc[...])
     coarse_apply(1)
     solved = ext[1, :, pl.ds(0, A1)]
     solved = solved + damping * (crhs[...] - (cst8 * solved + folded())) / cst8
     y2[...] = solved
     csol[...] = solved[0:6]
-    csol_out = pltpu.make_async_copy(csol, csol_h, out_sem.at[FX])
-    csol_out.start()
 
     entries = table(y2[...])
     tables = [y2[:, pl.ds(LANES * h, LANES)] for h in range(A1 // LANES)]
@@ -712,10 +714,6 @@
         values = smoothed(5, x)
         for c in range(3):
             sol[c, x] = values[c]
-        sol_out(x).start()
-
-    def sol_out(x):
-        return pltpu.make_async_copy(sol.at[:, x], sol_h.at[:, x], out_sem.at[x])
 
     inside(5)
     wait_halo(5)
@@ -744,14 +742,13 @@
             def _():
                 to_part(at, 0).wait_send()
 
-    for x in range(FX):
-        sol_out(x).wait()
-    csol_out.wait()
-
-
-def write_out(sol, csol, sol_out, csol_out):
-    sol_out[...] = sol[...]
-    csol_out[...] = csol[...]
+
+def write_out(sol, csol, sol_h, csol_h, sem):
+    copies = [pltpu.make_async_copy(sol, sol_h, sem.at[0]), pltpu.make_async_copy(csol, csol_h, sem.at[1])]
+    for copy in copies:
+        copy.start()
+    for copy in copies:
+        copy.wait()
 
 
 def body(nx, ny, rhs, stiffness, couplings, tentative, members, cst, ccp, col, snd, ctn, cmb, inv):
@@ -781,8 +778,6 @@
         pltpu.VMEM((40, A1 + 4 * H), F32),
         pltpu.VMEM((4, 40, H), F32),
         pltpu.VMEM((2, *inv.shape), BF16),
-        pltpu.VMEM((3, FX, FY, NZ), F32),
-        pltpu.VMEM((6, A1), F32),
         pltpu.VMEM((FX, LANES, FY * NZ), BF16),
         pltpu.VMEM((K, LANES, A1), BF16),
         pltpu.VMEM((1, 2 * LANES), F32),
@@ -791,7 +786,6 @@
         pltpu.VMEM((3, nx, 1, 2 * LANES), F32),
         pltpu.SemaphoreType.REGULAR((3,)),
         dma((18,)),
-        dma((FX + 1,)),
         dma((FIELDS, 4)),
         dma((FIELDS, 4)),
         dma((2, 4)),
@@ -803,12 +797,9 @@
     ]
     results = pl.pallas_call(
         functools.partial(kernel, nx, ny),
-        out_shape=(
-            jax.ShapeDtypeStruct((3, FX, FY, NZ), F32),
-            jax.ShapeDtypeStruct((6, A1), F32),
-        ),
+        out_shape=(pltpu.VMEM((3, FX, FY, NZ), F32), pltpu.VMEM((6, A1), F32)),
         in_specs=[pl.BlockSpec(memory_space=pl.ANY)] * len(operands),
-        out_specs=(pl.BlockSpec(memory_space=pl.ANY),) * 2,
+        out_specs=(pl.BlockSpec(memory_space=pltpu.VMEM),) * 2,
         scratch_shapes=scratch,
         compiler_params=pltpu.CompilerParams(
             collective_id=0, has_side_effects=True, vmem_limit_bytes=56 * 1024 * 1024
@@ -818,9 +809,10 @@
         write_out,
         out_shape=tuple(jax.ShapeDtypeStruct(result.shape, result.dtype) for result in results),
         in_specs=[pl.BlockSpec(memory_space=pltpu.VMEM)] * 2,
-        out_specs=(pl.BlockSpec(memory_space=pltpu.VMEM),) * 2,
+        out_specs=(pl.BlockSpec(memory_space=pl.ANY),) * 2,
+        scratch_shapes=[dma((2,))],
         compiler_params=pltpu.CompilerParams(vmem_limit_bytes=60 * 1024 * 1024),
-    )(*results)
+    )(*[pltpu.with_memory_space_constraint(result, pltpu.VMEM) for result in results])
 
 
 def solution(mesh):

time: 62.9 us -> 61.3 us (0.975)
  Pallas kernels: 62.2 us -> 60.6 us
    pallas_call x1, Pallas kernels: 1.77 us -> 0.77 us  [body(): pl.pallas_call(write_out, out_shape=tuple((jax.ShapeDtypeStruct(result.sh...]
where the time goes in v5:
time: 61.3 us; the launch traced here: 61.2 us
  Pallas kernels  60.6 us (99%)
  between operations  0.64 us (1%)
    pallas_call x1, Pallas kernels, body(): pl.pallas_call(functools.partial(kernel, nx, ny), out_shape=(pltpu.VMEM((...  59.8 us

profile of v5, /device:TPU:9, one launch (start us, length us, event | category | flops | bytes accessed | tf_op | source)
XLA Modules:
  0.0 61.2 jit_solution(5133962217294004126)
XLA Ops:
  0.6 59.8 %shard_map.131 = (f32[3,8,8,512]{3,2,1,0:T(8,128)S(1)}, f32[6,1024]{1,0:T(8,128)S(1)}) custom-call(f32[3,8,8,512]{3,2,1,0:T(8,128)} %rhs_h.1, f32[3,8,8,512]{3,2,1,0:T(8,128)} %stf_h.1, bf16[63,8,8,512]{3,2,1,0:T(8,128)(2,1)} %bitcast.3, bf16[18,8,8,512]{3,2,1,0:T(8,128)(2,1)} %bitcast.4, s32[8,8,512]{2,1,0:T(8,128)} %mem_h.1, f32[6,1024]{1,0:T(8,128)} %cst_h.1, ...), custom_call_target="tpu_custom_call" | custom-call | tf_op jit(solution)/shard_map/pallas_call | solution.py:798
  60.4 0.8 %shard_map.132 = (f32[3,8,8,512]{3,2,1,0:T(8,128)}, f32[6,1024]{1,0:T(8,128)}) custom-call(f32[3,8,8,512]{3,2,1,0:T(8,128)S(1)} %get-tuple-element.4.sol, f32[6,1024]{1,0:T(8,128)S(1)} %get-tuple-element.5.csol), custom_call_target="tpu_custom_call" | custom-call | tf_op jit(solution)/shard_map/pallas_call | solution.py:808

commit v6 on v5

--- a/solution.py
+++ b/solution.py
@@ -573,7 +573,8 @@
             device_id_type=MESH,
         )
 
-    for step in range(1, ny):
+    far_first = sorted(range(1, ny), key=lambda step: -min(step, ny - step))
+    for step in far_first:
         to_row(step).start()
     for step in range(1, ny):
         from_row(lax.rem(gy + step, ny)).wait_recv()
@@ -609,14 +610,20 @@
         other = lax.rem(gx + step, nx)
         return part(at, other, 0, {"gx": other, "gy": jnp.clip(gx + at - 1, 0, ny - 1)})
 
-    for at in (1, 0, 2):
-        target, held = gy + 1 - at, gx + at - 1
+    for steps in (far_first[: ny // 2], far_first[ny // 2 :]):
+        for at in (0, 2, 1):
+            target = gy + 1 - at
+
+            @pl.when(jnp.logical_and(target >= 0, target < nx))
+            def _():
+                for step in steps:
+                    to_part(at, step).start()
+
+    for at in (0, 2, 1):
+        target = gy + 1 - at
 
         @pl.when(jnp.logical_and(target >= 0, target < nx))
         def _():
-            for step in range(1, ny):
-                to_part(at, step).start()
-
             @pl.when(gx != target)
             def _():
                 to_part(at, 0).start()
@@ -626,7 +633,7 @@
                 parts[at, gx] = part_row[...]
 
     for at in (1, 0, 2):
-        target, held = gy + 1 - at, gx + at - 1
+        held = gx + at - 1
 
         @pl.when(jnp.logical_and(held >= 0, held < ny))
         def _():
@@ -691,6 +698,38 @@
 
     slabs(3, lift)
 
+    def sent_halos(first_number, last_number):
+        for side in range(4):
+
+            @pl.when(near[side][0])
+            def _():
+                for number in range(first_number, last_number):
+                    halo(number, side).wait_send()
+
+    def sent_lists():
+        for side in range(4):
+
+            @pl.when(near[side][0])
+            def _():
+                for number in range(2):
+                    coarse_halo(number, side ^ 1).wait_send()
+
+        for step in range(1, ny):
+            to_row(step).wait_send()
+
+    def sent_parts():
+        for at in range(3):
+            target = gy + 1 - at
+
+            @pl.when(jnp.logical_and(target >= 0, target < nx))
+            def _():
+                for step in range(1, ny):
+                    to_part(at, step).wait_send()
+
+                @pl.when(gx != target)
+                def _():
+                    to_part(at, 0).wait_send()
+
     def corrected(x):
         total = outside(3, x)
         put_field(
@@ -707,6 +746,8 @@
     slabs(4, corrected)
 
     inside(4)
+    sent_lists()
+    sent_halos(0, 4)
     wait_halo(4)
     slabs(5, lambda x: put_field(5, x, smoothed(4, x)))
 
@@ -716,31 +757,11 @@
             sol[c, x] = values[c]
 
     inside(5)
+    sent_parts()
     wait_halo(5)
     slabs(None, last)
 
-    for side in range(4):
-
-        @pl.when(near[side][0])
-        def _():
-            for number in range(FIELDS):
-                halo(number, side).wait_send()
-            for number in range(2):
-                coarse_halo(number, side ^ 1).wait_send()
-
-    for step in range(1, ny):
-        to_row(step).wait_send()
-    for at in range(3):
-        target = gy + 1 - at
-
-        @pl.when(jnp.logical_and(target >= 0, target < nx))
-        def _():
-            for step in range(1, ny):
-                to_part(at, step).wait_send()
-
-            @pl.when(gx != target)
-            def _():
-                to_part(at, 0).wait_send()
+    sent_halos(4, 6)
 
 
 def write_out(sol, csol, sol_h, csol_h, sem):

time: 61.3 us -> 61 us (level)
  no operation moved by 1% of the time
where the time goes in v6:
time: 61 us; the launch traced here: 60.9 us
  Pallas kernels  60.2 us (99%)
  between operations  0.64 us (1%)
    pallas_call x1, Pallas kernels, body(): pl.pallas_call(functools.partial(kernel, nx, ny), out_shape=(pltpu.VMEM((...  59.5 us

profile of v6, /device:TPU:9, one launch (start us, length us, event | category | flops | bytes accessed | tf_op | source)
XLA Modules:
  0.0 60.9 jit_solution(18371749136288182666)
XLA Ops:
  0.6 59.5 %shard_map.131 = (f32[3,8,8,512]{3,2,1,0:T(8,128)S(1)}, f32[6,1024]{1,0:T(8,128)S(1)}) custom-call(f32[3,8,8,512]{3,2,1,0:T(8,128)} %rhs_h.1, f32[3,8,8,512]{3,2,1,0:T(8,128)} %stf_h.1, bf16[63,8,8,512]{3,2,1,0:T(8,128)(2,1)} %bitcast.3, bf16[18,8,8,512]{3,2,1,0:T(8,128)(2,1)} %bitcast.4, s32[8,8,512]{2,1,0:T(8,128)} %mem_h.1, f32[6,1024]{1,0:T(8,128)} %cst_h.1, ...), custom_call_target="tpu_custom_call" | custom-call | tf_op jit(solution)/shard_map/pallas_call | solution.py:819
  60.1 0.8 %shard_map.132 = (f32[3,8,8,512]{3,2,1,0:T(8,128)}, f32[6,1024]{1,0:T(8,128)}) custom-call(f32[3,8,8,512]{3,2,1,0:T(8,128)S(1)} %get-tuple-element.4.sol, f32[6,1024]{1,0:T(8,128)S(1)} %get-tuple-element.5.csol), custom_call_target="tpu_custom_call" | custom-call | tf_op jit(solution)/shard_map/pallas_call | solution.py:829

commit v7 on v6

--- a/solution.py
+++ b/solution.py
@@ -429,9 +429,30 @@
 
     loads["ten"].wait()
 
-    def restrict(x):
-        total = outside(2, x)
-        filtered = [resid[i, x] - smoothing * total[i] for i in range(3)]
+    fine_row = lax.broadcasted_iota(jnp.int32, (FY, NZ), 0)
+
+    def restrict_own(x):
+        total = [acc[i, x] for i in range(3)]
+        for j in range(3):
+            view = field[2, j, x]
+            add(total, 3, x, j, jnp.where(fine_row == 0, 0.0, pltpu.roll(view, 1, axis=0)))
+            add(total, 4, x, j, jnp.where(fine_row == FY - 1, 0.0, pltpu.roll(view, FY - 1, axis=0)))
+        restrict(x, [resid[i, x] - smoothing * total[i] for i in range(3)])
+
+    def restrict_rest(x):
+        total = [jnp.zeros((FY, NZ), F32) for _ in range(3)]
+        for j in range(3):
+            below = yin[0, j, pl.ds(x, 1), :]
+            above = yin[1, j, pl.ds(x, 1), :]
+            add(total, 3, x, j, jnp.where(fine_row == 0, below, 0.0))
+            add(total, 4, x, j, jnp.where(fine_row == FY - 1, above, 0.0))
+            if isinstance(x, int) and x == 0:
+                add(total, 1, x, j, received(2, 0, j))
+            if isinstance(x, int) and x == FX - 1:
+                add(total, 2, x, j, received(2, 1, j))
+        restrict(x, [-smoothing * total[i] for i in range(3)])
+
+    def restrict(x, filtered):
         for c in range(6):
             value = ten[c, x].astype(F32) * filtered[0]
             for i in range(1, 3):
@@ -448,13 +469,10 @@
     invs[0] = rounded
     invs[1] = (whole - rounded.astype(F32)).astype(BF16)
     inside(2)
-    heard(2)
-    wait_halo(2)
-    wait_coarse(1)
-    slabs(None, restrict)
-
-    def sums(x, total):
-        for y in range(FY):
+    slabs(None, restrict_own)
+
+    def sums(x, total, ys):
+        for y in ys:
             value = jnp.concatenate(
                 [nodes[x, t, pl.ds(y, 8, stride=8), :] for t in range(NZ // LANES)], axis=1
             )
@@ -470,7 +488,15 @@
             )
         return total
 
-    gathered = lax.fori_loop(0, FX, sums, jnp.zeros((LANES, LANES), F32))
+    gathered = lax.fori_loop(
+        0, FX, lambda x, total: sums(x, total, range(FY)), jnp.zeros((16 * A1 // LANES, LANES), F32)
+    )
+    heard(2)
+    wait_halo(2)
+    wait_coarse(1)
+    slabs(None, restrict_rest)
+    gathered = sums(FX - 1, sums(0, gathered, range(FY)), range(FY))
+    gathered = lax.fori_loop(1, FX - 1, lambda x, total: sums(x, total, (0, FY - 1)), gathered)
 
     loads["cst"].wait()
     for h in range(8):

time: 61 us -> 61.3 us (level); the launches traced: 60.9 us -> 60.4 us
  no operation moved by 1% of the time
where the time goes in v7:
time: 61.3 us; the launch traced here: 60.4 us
  Pallas kernels  59.7 us (97%)
  between operations  0.64 us (1%)
    pallas_call x1, Pallas kernels, body(): pl.pallas_call(functools.partial(kernel, nx, ny), out_shape=(pltpu.VMEM((...  59 us

profile of v7, /device:TPU:9, one launch (start us, length us, event | category | flops | bytes accessed | tf_op | source)
XLA Modules:
  0.0 60.4 jit_solution(12613274023678021905)
XLA Ops:
  0.6 59.0 %shard_map.131 = (f32[3,8,8,512]{3,2,1,0:T(8,128)S(1)}, f32[6,1024]{1,0:T(8,128)S(1)}) custom-call(f32[3,8,8,512]{3,2,1,0:T(8,128)} %rhs_h.1, f32[3,8,8,512]{3,2,1,0:T(8,128)} %stf_h.1, bf16[63,8,8,512]{3,2,1,0:T(8,128)(2,1)} %bitcast.3, bf16[18,8,8,512]{3,2,1,0:T(8,128)(2,1)} %bitcast.4, s32[8,8,512]{2,1,0:T(8,128)} %mem_h.1, f32[6,1024]{1,0:T(8,128)} %cst_h.1, ...), custom_call_target="tpu_custom_call" | custom-call | tf_op jit(solution)/shard_map/pallas_call | solution.py:845
  59.6 0.8 %shard_map.132 = (f32[3,8,8,512]{3,2,1,0:T(8,128)}, f32[6,1024]{1,0:T(8,128)}) custom-call(f32[3,8,8,512]{3,2,1,0:T(8,128)S(1)} %get-tuple-element.4.sol, f32[6,1024]{1,0:T(8,128)S(1)} %get-tuple-element.5.csol), custom_call_target="tpu_custom_call" | custom-call | tf_op jit(solution)/shard_map/pallas_call | solution.py:855
